TPU v7x, 512 devices: a whole 4x8x8 slice. The times are simulated.
512 devices in a mesh: cp: 64 (over z_hi, y, core), tp: 8 (over x, z_lo).
Axes of the slice: x: 4, y: 8, z: 8 (z_hi: 4, z_lo: 2; z = z_hi * 2 + z_lo), core: 2. Of those that a mesh axis runs over, the one named last changes fastest.
Arguments:
- query_rows: bfloat16 [128, 256, 8192], P('cp', 'tp'), may hold values from -6 to 6
- key_rows: bfloat16 [128, 256, 1024], P('cp', 'tp'), may hold values from -6 to 6
- value_matrix: bfloat16 [128, 256, 1024], P('cp', 'tp'), may hold values from -6 to 6
- doc_start: int32 [128, 256], P('cp'), may hold values from 0 to 32767, as said below
- source_lists: int32 [128, 2], P('cp'), may hold values from -1 to 126, as said below
- slot_block: int32 [128], replicated, may hold values from 0 to 127, as said below
Outputs:
- attended: bfloat16 [128, 256, 8192], P('cp', None, 'tp')
Inputs may be any that keep to these rules, and one draw needn't show every extreme that they name: Documents lie end to end over the 32768 positions, each of 1 to 512 tokens and at least one of exactly 512; doc_start is constant within a document and equals the position of its first token. `source_lists`: the list of block b is b - 1, b - 2, ... down to the block that holds the document start of b's first token, then -1 to the end; some block names exactly 2 blocks. `slot_block`: cp device c holds blocks c and 127 - c in its 2 slots, in an order that is drawn for each device.
All inputs are finite; a program needn't handle non-finite values.
Results may differ from a plain program's by a relative error of at most 0.0035.
Values may be sent and summed in bfloat16 or wider, within the bound.
A program may use at most 64 MiB of HBM per device.

v0:
```python
import jax
import jax.numpy as jnp
from jax import lax
from jax.sharding import PartitionSpec as P

QUERY_HEAD_COUNT = 64
KEY_VALUE_HEADS = 8
HEAD_SIZE = 128
LIST = 2


neg_large = -1e30


def from_behind(block, axis, distance):
    devices = range(lax.axis_size(axis))
    route = [(i - distance, i) for i in devices if i - distance in devices]
    return lax.ppermute(block, axis, route)


def tile_update(carry, query_fourth, key_block, value_block, query_pos, starts, key_start):
    best, total, accum = carry
    token_list, groups_kv, query_group, width = query_fourth.shape
    key_third = key_block.reshape(token_list, groups_kv, width)
    value_third = value_block.reshape(token_list, groups_kv, width)
    scores = jnp.einsum(
        "qagd,kad->agqk", query_fourth, key_third, preferred_element_type=jnp.float32
    ) * width ** (-0.5)
    key_pos = key_start + jnp.arange(token_list, dtype=jnp.int32)
    visible = (key_pos[None, :] <= query_pos[:, None]) & (key_pos[None, :] >= starts[:, None])
    scores = jnp.where(visible[None, None], scores, neg_large)
    newest = jnp.maximum(best, jnp.max(scores, axis=-1))
    weights = jnp.exp(scores - newest[..., None])
    scale_factor = jnp.exp(best - newest)
    total = total * scale_factor + jnp.sum(weights, axis=-1)
    update = jnp.einsum(
        "agqk,kad->agqd",
        weights.astype(jnp.bfloat16),
        value_third,
        preferred_element_type=jnp.float32,
    )
    accum = accum * scale_factor[..., None] + update
    return (newest, total, accum)


def on_device(query_rows, key_rows, value_matrix, doc_start, source_lists, slot_block):
    held = query_rows.shape[0]
    query_heads, key_heads, value_heads = (
        lax.all_to_all(query_rows, "tp", split_axis=2, concat_axis=1, tiled=True),
        lax.all_to_all(key_rows, "tp", split_axis=2, concat_axis=1, tiled=True),
        lax.all_to_all(value_matrix, "tp", split_axis=2, concat_axis=1, tiled=True),
    )
    token_list = query_heads.shape[1]
    kv_width = key_heads.shape[2]
    groups_kv = kv_width // HEAD_SIZE
    query_group = QUERY_HEAD_COUNT // KEY_VALUE_HEADS
    device_index = lax.axis_index("cp")
    paired = jnp.stack([key_heads, value_heads])
    below = []
    above = []
    for distance in range(1, LIST + 1):
        below.append(from_behind(paired, "cp", distance))
        above.append(from_behind(paired, "cp", -distance))
    gathered = jnp.stack(below[::-1] + [paired] + above)
    key_stack = gathered[:, 0].reshape(-1, token_list, kv_width)
    value_stack = gathered[:, 1].reshape(-1, token_list, kv_width)
    slot_ids = jnp.arange(slot_block.shape[0], dtype=jnp.int32)
    offsets = jnp.arange(token_list, dtype=jnp.int32)
    outputs = []
    for place in range(held):
        block_id = slot_block[device_index * held + place]
        query_fourth = query_heads[place].reshape(token_list, groups_kv, query_group, HEAD_SIZE)
        query_pos = block_id * token_list + offsets
        starts = doc_start[place]
        shape_rows = (groups_kv, query_group, token_list)
        carry = (
            jnp.full(shape_rows, neg_large, jnp.float32),
            jnp.zeros(shape_rows, jnp.float32),
            jnp.zeros(shape_rows + (HEAD_SIZE,), jnp.float32),
        )
        carry = tile_update(
            carry,
            query_fourth,
            key_heads[place],
            value_heads[place],
            query_pos,
            starts,
            block_id * token_list,
        )
        listed = source_lists[place]
        listed_count = jnp.sum((listed >= 0).astype(jnp.int32))

        def visit(
            entry,
            state,
            listed=listed,
            query_fourth=query_fourth,
            query_pos=query_pos,
            starts=starts,
        ):
            source = listed[entry]
            holder = jnp.sum(jnp.where(slot_block == source, slot_ids, 0))
            stack_index = (LIST + holder // held - device_index) * held + holder % held
            key_block = lax.dynamic_index_in_dim(key_stack, stack_index, 0, keepdims=False)
            value_block = lax.dynamic_index_in_dim(value_stack, stack_index, 0, keepdims=False)
            return tile_update(
                state, query_fourth, key_block, value_block, query_pos, starts, source * token_list
            )

        best, total, accum = lax.fori_loop(0, listed_count, visit, carry)
        mixed = accum / total[..., None]
        outputs.append(
            jnp.transpose(mixed, (2, 0, 1, 3))
            .reshape(token_list, groups_kv * query_group * HEAD_SIZE)
            .astype(jnp.bfloat16)
        )
    return jnp.stack(outputs)


def solution(mesh):
    in_specs = (
        P("cp", "tp", None),
        P("cp", "tp", None),
        P("cp", "tp", None),
        P("cp", None),
        P("cp", None),
        P(),
    )
    out_specs = P("cp", None, "tp")
    return jax.shard_map(
        on_device, mesh=mesh, in_specs=in_specs, out_specs=out_specs, check_vma=False
    )
```

profile of v0, /device:TPU:254, one launch (start us, length us, event | category | flops | bytes accessed | tf_op | source)
XLA Modules:
  0.0 125.5 jit_solution(15800691529196060555)
XLA Ops:
  0.0 1.3 %copy.38 = bf16[2,32,1024]{1,0,2:T(2,128)(2,1)S(1)} copy(bf16[2,32,1024]{2,1,0:T(8,128)(2,1)} %param.11) | data formatting | bytes 262144 | tf_op args[1]
  1.3 1.2 reshape.600
  2.5 5.7 %all-to-all-start = ((bf16[8,2,4096]{2,1,0:T(2,128)(2,1)}), bf16[8,2,4096]{2,1,0:T(2,128)(2,1)S(1)}, u32[]{:S(2)}, u32[]{:S(2)}) async-start(bf16[8,2,4096]{2,1,0:T(2,128)(2,1)} %reshape.600), calls=%async_computation | async-start | bytes 262144 | tf_op jit(solution)/shard_map/all_to_all | solution.py:50
  8.1 1.5 %fusion.54 = (s32[]{:T(128)}, s32[]{:T(128)}) fusion(s32[2,2]{1,0:T(2,128)} %param.14), kind=kLoop, calls=%fused_computation.93 | loop fusion | flops 10 | bytes 24 | tf_op jit(solution)/shard_map/reduce_sum | solution.py:91
  9.6 1.3 %slice_bitcast_fusion.1 = (s32[2]{0:T(128)}, s32[2]{0:T(128)}) fusion(s32[2,2]{1,0:T(2,128)} %param.14), kind=kLoop, calls=%fused_computation.96 | loop fusion | bytes 32 | tf_op jit(solution)/shard_map/squeeze | solution.py:90
  10.9 0.8 fusion.64
  11.7 1.4 %fusion.65 = (s32[1]{0:T(128)}, s32[1]{0:T(128)}) fusion(s32[128]{0:T(128)} %param.15, s32[]{:T(128)S(6)} %select_n.100, s32[]{:T(128)S(6)} %select_n.102), kind=kLoop, calls=%fused_computation.106 | loop fusion | bytes 24 | tf_op jit(solution)/shard_map/dynamic_slice | solution.py:71
  13.7 1.2 copy.43
  14.9 1.2 reshape.604
  16.9 5.7 %all-to-all-start.2 = ((bf16[8,2,4096]{2,1,0:T(2,128)(2,1)}), bf16[8,2,4096]{2,1,0:T(2,128)(2,1)S(1)}, u32[]{:S(2)}, u32[]{:S(2)}) async-start(bf16[8,2,4096]{2,1,0:T(2,128)(2,1)} %reshape.604), calls=%async_computation.2 | async-start | bytes 262144 | tf_op jit(solution)/shard_map/all_to_all | solution.py:51
  22.6 6.8 %copy.40 = bf16[2,32,8192]{1,0,2:T(2,128)(2,1)} copy(bf16[2,32,8192]{2,1,0:T(8,128)(2,1)S(1)} %copy-done) | data formatting | bytes 2097152 | tf_op args[0]
  29.5 7.8 %reshape.602 = bf16[8,2,32768]{2,1,0:T(2,128)(2,1)} reshape(bf16[8192,2,32]{2,1,0:T(2,128)(2,1)} %bitcast.239) | data formatting | bytes 2097152
  37.7 0.4 copy.39
  38.1 5.7 %all-to-all-start.1 = ((bf16[8,2,32768]{2,1,0:T(2,128)(2,1)}), bf16[8,2,32768]{2,1,0:T(2,128)(2,1)S(1)}, u32[]{:S(2)}, u32[]{:S(2)}) async-start(bf16[8,2,32768]{2,1,0:T(2,128)(2,1)} %reshape.602), calls=%async_computation.1 | async-start | bytes 2097152 | tf_op jit(solution)/shard_map/all_to_all | solution.py:49
  44.1 0.4 copy.44
  44.5 5.6 %collective-permute-start = (bf16[2,2,256,128]{3,2,1,0:T(8,128)(2,1)S(1)}, bf16[2,2,256,128]{3,2,1,0:T(8,128)(2,1)S(1)}, u32[]{:S(2)}, u32[]{:S(2)}) collective-permute-start(bf16[2,2,256,128]{3,2,1,0:T(8,128)(2,1)S(1)} %pad_maximum_fusion.1), channel_id=1, source_target_pairs={{0,16},{8,24},{16,32},{24,40},{32,48},{40,56},{48,64},{56,72},{64,... | collective-permute-start | bytes 786440 | tf_op jit(solution)/shard_map/ppermute | solution.py:18
  50.1 1.9 %collective-permute-start.1 = (bf16[2,2,256,128]{3,2,1,0:T(8,128)(2,1)S(1)}, bf16[2,2,256,128]{3,2,1,0:T(8,128)(2,1)S(1)}, u32[]{:S(2)}, u32[]{:S(2)}) collective-permute-start(bf16[2,2,256,128]{3,2,1,0:T(8,128)(2,1)S(1)} %pad_maximum_fusion.1), channel_id=1, source_target_pairs={{0,8},{8,16},{16,24},{24,32},{32,40},{40,48},{48,56},{56,64},{64,7... | collective-permute-start | bytes 786440 | tf_op jit(solution)/shard_map/ppermute | solution.py:18
  52.0 3.6 %collective-permute-start.2 = (bf16[2,2,256,128]{3,2,1,0:T(8,128)(2,1)S(1)}, bf16[2,2,256,128]{3,2,1,0:T(8,128)(2,1)S(1)}, u32[]{:S(2)}, u32[]{:S(2)}) collective-permute-start(bf16[2,2,256,128]{3,2,1,0:T(8,128)(2,1)S(1)} %pad_maximum_fusion.1), channel_id=1, source_target_pairs={{8,0},{16,8},{24,16},{32,24},{40,32},{48,40},{56,48},{64,56},{72,6... | collective-permute-start | bytes 786440 | tf_op jit(solution)/shard_map/ppermute | solution.py:18
  55.7 1.9 %collective-permute-start.3 = (bf16[2,2,256,128]{3,2,1,0:T(8,128)(2,1)S(1)}, bf16[2,2,256,128]{3,2,1,0:T(8,128)(2,1)S(1)}, u32[]{:S(2)}, u32[]{:S(2)}) collective-permute-start(bf16[2,2,256,128]{3,2,1,0:T(8,128)(2,1)S(1)} %pad_maximum_fusion.1), channel_id=1, source_target_pairs={{16,0},{24,8},{32,16},{40,24},{48,32},{56,40},{64,48},{72,56},{80,... | collective-permute-start | bytes 786440 | tf_op jit(solution)/shard_map/ppermute | solution.py:18
  57.6 0.7 fusion.63
  58.3 0.7 fusion.62
  59.1 1.8 %collective-permute-done.2 = bf16[2,2,256,128]{3,2,1,0:T(8,128)(2,1)S(1)} collective-permute-done((bf16[2,2,256,128]{3,2,1,0:T(8,128)(2,1)S(1)}, bf16[2,2,256,128]{3,2,1,0:T(8,128)(2,1)S(1)}, u32[]{:S(2)}, u32[]{:S(2)}) %collective-permute-start.2) | collective-permute-done | bytes 262176 | tf_op jit(solution)/shard_map/ppermute | solution.py:18
  61.0 18.5 %collective-permute-done.3 = bf16[2,2,256,128]{3,2,1,0:T(8,128)(2,1)S(1)} collective-permute-done((bf16[2,2,256,128]{3,2,1,0:T(8,128)(2,1)S(1)}, bf16[2,2,256,128]{3,2,1,0:T(8,128)(2,1)S(1)}, u32[]{:S(2)}, u32[]{:S(2)}) %collective-permute-start.3) | collective-permute-done | bytes 262176 | tf_op jit(solution)/shard_map/ppermute | solution.py:18
  79.6 4.5 %reshape.603 = bf16[8192,2,32]{2,1,0:T(2,128)(2,1)} reshape(bf16[8,2,32768]{2,1,0:T(2,128)(2,1)S(1)} %all-to-all-done.1) | data formatting | bytes 2097152
  84.1 9.0 %copy.41 = bf16[2,32,8,1024]{3,1,2,0:T(8,128)(2,1)S(1)} copy(bf16[2,32,8,1024]{1,0,3,2:T(2,128)(2,1)} %bitcast.238) | data formatting | bytes 2097152 | tf_op jit(solution)/shard_map/all_to_all | solution.py:49
  93.3 0.6 copy-done.4
  94.0 0.5 fusion.67
  94.9 0.4 copy-done.3
  95.3 0.8 fusion.43
  96.1 15.5 %while.34 = (s32[]{:T(128)}, f32[1,8,256]{2,1,0:T(8,128)S(1)}, f32[1,8,256]{2,1,0:T(8,128)S(1)}, f32[1,8,256,128]{3,2,1,0:T(8,128)S(1)}, s32[]{:T(128)}, /*index...) while((s32[]{:T(128)}, f32[1,8,256]{2,1,0:T(8,128)S(1)}, ...), condition=%wide.region_7.8_spmd.clone, body=%wide.region_3.7_spmd.clone.sunk | while | flops 272833440 | bytes 9312268 | solution.py:110
  96.7 0.6 dynamic_slice.81
  97.3 1.3 %fusion.88 = s32[]{:T(128)} fusion(s32[128]{0:T(128)S(1)} %get-tuple-element.859, s32[]{:T(128)} %bitcast.225), kind=kLoop, calls=%fused_computation.25.clone.1 | loop fusion | flops 383 | bytes 520 | tf_op jit(solution)/shard_map/while/body/reduce_sum | solution.py:102
  101.7 0.5 fusion.89
  102.2 1.0 fusion.92
  104.2 0.6 dynamic_slice.81
  104.8 1.3 %fusion.88 = s32[]{:T(128)} fusion(s32[128]{0:T(128)S(1)} %get-tuple-element.859, s32[]{:T(128)} %bitcast.225), kind=kLoop, calls=%fused_computation.25.clone.1 | loop fusion | flops 383 | bytes 520 | tf_op jit(solution)/shard_map/while/body/reduce_sum | solution.py:102
  109.1 0.5 fusion.89
  109.6 1.0 fusion.92
  112.0 0.3 copy.51
  112.7 0.5 fusion.66
  113.6 0.4 copy-done.1
  114.0 0.8 fusion.42
  114.8 8.7 %while.35 = (s32[]{:T(128)}, f32[1,8,256]{2,1,0:T(8,128)S(1)}, f32[1,8,256]{2,1,0:T(8,128)S(1)}, f32[1,8,256,128]{3,2,1,0:T(8,128)S(1)}, s32[]{:T(128)}, /*index...) while((s32[]{:T(128)}, f32[1,8,256]{2,1,0:T(8,128)S(1)}, ...), condition=%wide.region_15.16_spmd.clone, body=%wide.region_11.15_spmd.clone.sunk | while | flops 272833440 | bytes 9312268 | solution.py:110
  115.7 0.6 dynamic_slice.84
  116.2 1.3 %fusion.95 = s32[]{:T(128)} fusion(s32[128]{0:T(128)S(1)} %get-tuple-element.802, s32[]{:T(128)} %bitcast.235), kind=kLoop, calls=%fused_computation.49.clone.1 | loop fusion | flops 383 | bytes 520 | tf_op jit(solution)/shard_map/while/body/reduce_sum | solution.py:102
  120.9 0.5 fusion.96
  121.4 1.0 fusion.99
  124.4 1.1 pad_maximum_fusion
  (73 shorter events, 5.1 us)
Async XLA Ops:
  0.0 22.6 %copy-start = (bf16[2,32,8192]{2,1,0:T(8,128)(2,1)S(1)}, bf16[2,32,8192]{2,1,0:T(8,128)(2,1)}, u32[]{:S(2)}) copy-start(bf16[2,32,8192]{2,1,0:T(8,128)(2,1)} %param.10) | copy-start | bytes 3145732
  2.5 14.4 %all-to-all-start = ((bf16[8,2,4096]{2,1,0:T(2,128)(2,1)}), bf16[8,2,4096]{2,1,0:T(2,128)(2,1)S(1)}, u32[]{:S(2)}, u32[]{:S(2)}) async-start(bf16[8,2,4096]{2,1,0:T(2,128)(2,1)} %reshape.600), calls=%async_computation | async-start | bytes 262144 | tf_op jit(solution)/shard_map/all_to_all | solution.py:50
  11.7 17.8 %copy-start.7 = (s32[1,256]{1,0:T(1,128)}, s32[1,256]{1,0:T(1,128)S(1)}, u32[]{:S(2)}) copy-start(s32[1,256]{1,0:T(1,128)S(1)} %get-tuple-element.820) | copy-start | bytes 3076
  11.7 25.6 %copy-start.5 = (s32[1,256]{1,0:T(1,128)}, s32[1,256]{1,0:T(1,128)S(1)}, u32[]{:S(2)}) copy-start(s32[1,256]{1,0:T(1,128)S(1)} %get-tuple-element.763) | copy-start | bytes 3076
  16.9 21.2 %all-to-all-start.2 = ((bf16[8,2,4096]{2,1,0:T(2,128)(2,1)}), bf16[8,2,4096]{2,1,0:T(2,128)(2,1)S(1)}, u32[]{:S(2)}, u32[]{:S(2)}) async-start(bf16[8,2,4096]{2,1,0:T(2,128)(2,1)} %reshape.604), calls=%async_computation.2 | async-start | bytes 262144 | tf_op jit(solution)/shard_map/all_to_all | solution.py:51
  38.1 41.6 %all-to-all-start.1 = ((bf16[8,2,32768]{2,1,0:T(2,128)(2,1)}), bf16[8,2,32768]{2,1,0:T(2,128)(2,1)S(1)}, u32[]{:S(2)}, u32[]{:S(2)}) async-start(bf16[8,2,32768]{2,1,0:T(2,128)(2,1)} %reshape.602), calls=%async_computation.1 | async-start | bytes 2097152 | tf_op jit(solution)/shard_map/all_to_all | solution.py:49
  44.5 14.6 %collective-permute-start = (bf16[2,2,256,128]{3,2,1,0:T(8,128)(2,1)S(1)}, bf16[2,2,256,128]{3,2,1,0:T(8,128)(2,1)S(1)}, u32[]{:S(2)}, u32[]{:S(2)}) collective-permute-start(bf16[2,2,256,128]{3,2,1,0:T(8,128)(2,1)S(1)} %pad_maximum_fusion.1), channel_id=1, source_target_pairs={{0,16},{8,24},{16,32},{24,40},{32,48},{40,56},{48,64},{56,72},{64,... | collective-permute-start | bytes 786440 | tf_op jit(solution)/shard_map/ppermute | solution.py:18
  50.1 9.0 %collective-permute-start.1 = (bf16[2,2,256,128]{3,2,1,0:T(8,128)(2,1)S(1)}, bf16[2,2,256,128]{3,2,1,0:T(8,128)(2,1)S(1)}, u32[]{:S(2)}, u32[]{:S(2)}) collective-permute-start(bf16[2,2,256,128]{3,2,1,0:T(8,128)(2,1)S(1)} %pad_maximum_fusion.1), channel_id=1, source_target_pairs={{0,8},{8,16},{16,24},{24,32},{32,40},{40,48},{48,56},{56,64},{64,7... | collective-permute-start | bytes 786440 | tf_op jit(solution)/shard_map/ppermute | solution.py:18
  52.0 8.9 %collective-permute-start.2 = (bf16[2,2,256,128]{3,2,1,0:T(8,128)(2,1)S(1)}, bf16[2,2,256,128]{3,2,1,0:T(8,128)(2,1)S(1)}, u32[]{:S(2)}, u32[]{:S(2)}) collective-permute-start(bf16[2,2,256,128]{3,2,1,0:T(8,128)(2,1)S(1)} %pad_maximum_fusion.1), channel_id=1, source_target_pairs={{8,0},{16,8},{24,16},{32,24},{40,32},{48,40},{56,48},{64,56},{72,6... | collective-permute-start | bytes 786440 | tf_op jit(solution)/shard_map/ppermute | solution.py:18
  55.7 23.8 %collective-permute-start.3 = (bf16[2,2,256,128]{3,2,1,0:T(8,128)(2,1)S(1)}, bf16[2,2,256,128]{3,2,1,0:T(8,128)(2,1)S(1)}, u32[]{:S(2)}, u32[]{:S(2)}) collective-permute-start(bf16[2,2,256,128]{3,2,1,0:T(8,128)(2,1)S(1)} %pad_maximum_fusion.1), channel_id=1, source_target_pairs={{16,0},{24,8},{32,16},{40,24},{48,32},{56,40},{64,48},{72,56},{80,... | collective-permute-start | bytes 786440 | tf_op jit(solution)/shard_map/ppermute | solution.py:18
  93.1 0.8 copy-start.4
  94.4 0.8 copy-start.3
  94.8 1.3 %copy-start.8 = (s32[1,256]{1,0:T(1,128)S(1)}, s32[1,256]{1,0:T(1,128)}, u32[]{:S(2)}) copy-start(s32[1,256]{1,0:T(1,128)} %copy-done.7) | copy-start | bytes 3076
  94.8 1.3 %copy-start.9 = (s32[128]{0:T(128)S(1)}, s32[128]{0:T(128)}, u32[]{:S(2)}) copy-start(s32[128]{0:T(128)} %param.15) | copy-start | bytes 1540
  94.8 1.3 %copy-start.11 = (s32[2]{0:T(128)S(1)}, s32[2]{0:T(128)}, u32[]{:S(2)}) copy-start(s32[2]{0:T(128)} %get-tuple-element.819) | copy-start | bytes 28
  111.6 1.0 copy-start.2
  113.1 0.8 copy-start.1
  113.5 1.3 %copy-start.6 = (s32[1,256]{1,0:T(1,128)S(1)}, s32[1,256]{1,0:T(1,128)}, u32[]{:S(2)}) copy-start(s32[1,256]{1,0:T(1,128)} %copy-done.5) | copy-start | bytes 3076
  113.5 1.3 %copy-start.10 = (s32[2]{0:T(128)S(1)}, s32[2]{0:T(128)}, u32[]{:S(2)}) copy-start(s32[2]{0:T(128)} %get-tuple-element.762) | copy-start | bytes 28
where the time goes:
time: 127 us; the launch traced here: 125 us
  local copies, waits for them, and re-layouts  44 us (35%)
  starting transfers between devices  30.2 us (24%)
  waiting for transfers between devices  20.4 us (16%)
  loops' own time  12.7 us (10%)
  other arithmetic  9.34 us (7%)
  matrix products  7.01 us (6%)
  between operations  1.81 us (1%)
    unnamed x40, local copies, waits for them, and re-layouts  26.4 us
    ppermute x4, waiting for transfers between devices, from_behind(): return lax.ppermute(block, axis, route)  20.4 us
    ppermute x4, starting transfers between devices, from_behind(): return lax.ppermute(block, axis, route)  13.1 us
    another operation x2, loops' own time, on_device(): best, total, accum = lax.fori_loop(0, listed_count, visit, carry)  12.7 us
    all_to_all x1, local copies, waits for them, and re-layouts, on_device(): lax.all_to_all(query_rows, 'tp', split_axis=2, concat_axis=1, tiled=True)  8.96 us
    all_to_all x1, starting transfers between devices, on_device(): lax.all_to_all(value_matrix, 'tp', split_axis=2, concat_axis=1, tiled=True)  5.71 us
    all_to_all x1, starting transfers between devices, on_device(): lax.all_to_all(query_rows, 'tp', split_axis=2, concat_axis=1, tiled=True)  5.71 us
    all_to_all x1, starting transfers between devices, on_device(): lax.all_to_all(key_rows, 'tp', split_axis=2, concat_axis=1, tiled=True)  5.68 us
  transfers between devices with their start and end apart: 7, of which 3 were waited for; matrix products, arithmetic and copies ran while one was open for 20% of the time, Pallas kernels for 0%

commit v1 on v0

v1 whole, which is shorter than its diff:
```python
import functools

import jax
import jax.numpy as jnp
from jax import lax
from jax.experimental import pallas as pl
from jax.experimental.pallas import tpu as pltpu
from jax.sharding import PartitionSpec as P

QUERY_HEAD_COUNT = 64
KEY_VALUE_HEADS = 8
HEAD_SIZE = 128
LIST = 2
MESH = pl.DeviceIdType.MESH

neg_large = -1e30
SCALE = HEAD_SIZE ** (-0.5) * 1.4426950408889634
RUN = 2
ORDER = (0, 1, 2, 3, 6, 7, 4, 5)


def kernel(
    n_cp,
    n_tp,
    q_hbm,
    k_hbm,
    v_hbm,
    start_hbm,
    list_hbm,
    slot_hbm,
    out_hbm,
    q_all,
    k_all,
    v_all,
    stage,
    inbox,
    out_buf,
    start_buf,
    low_bound,
    list_buf,
    slot_buf,
    small_sem,
    own_sem,
    kv_send,
    kv_recv,
    q_send,
    q_recv,
    far_send,
    far_recv,
    out_sem,
):
    held, part, _ = q_hbm.shape
    tokens = part * n_tp
    width = q_hbm.shape[2] // n_tp
    kv_width = k_hbm.shape[2] // n_tp
    group = width // HEAD_SIZE
    window = LIST * tokens + tokens // 2
    c = lax.axis_index("cp")
    t = lax.axis_index("tp")
    n_x = n_tp // RUN
    x, z = t // RUN, t % RUN

    def peer(offset, sign):
        dx, dz = offset // RUN, offset % RUN
        return ((x + sign * dx + n_x) % n_x) * RUN + (z + sign * dz + RUN) % RUN

    barrier = pltpu.get_barrier_semaphore()
    for offset in range(1, n_tp):
        pl.semaphore_signal(
            barrier, inc=1, device_id=(c, peer(offset, 1)), device_id_type=MESH
        )
    for step in (1, 2):
        for side in (-1, 1):
            other = c + side * step

            @pl.when((other >= 0) & (other < n_cp))
            def _():
                pl.semaphore_signal(barrier, inc=1, device_id=(other, t), device_id_type=MESH)

    small = [
        pltpu.make_async_copy(start_hbm, start_buf, small_sem.at[0]),
        pltpu.make_async_copy(list_hbm, list_buf, small_sem.at[1]),
        pltpu.make_async_copy(slot_hbm, slot_buf, small_sem.at[2]),
    ]
    own_rows = pl.ds(pl.multiple_of(t * part, part), part)
    own_key_rows = pl.ds(pl.multiple_of(LIST * tokens + t * part, part), part)

    def cut(ref, size, which):
        return ref.at[:, :, pl.ds(pl.multiple_of(which * size, size), size)]

    own = [
        pltpu.make_async_copy(cut(q_hbm, width, t), q_all.at[:, own_rows], own_sem.at[0]),
        pltpu.make_async_copy(cut(k_hbm, kv_width, t), k_all.at[:, own_key_rows], own_sem.at[1]),
        pltpu.make_async_copy(cut(v_hbm, kv_width, t), v_all.at[:, own_key_rows], own_sem.at[2]),
    ]
    for copy in small + own:
        copy.start()

    greeted = n_tp - 1
    for step in (1, 2):
        greeted = greeted + jnp.where(c >= step, 1, 0) + jnp.where(c + step < n_cp, 1, 0)
    pl.semaphore_wait(barrier, greeted)

    kv_copies = []
    q_copies = {}
    for offset in range(1, n_tp):
        to = peer(offset, 1)
        for which, (ref, dst) in enumerate(((k_hbm, k_all), (v_hbm, v_all))):
            kv_copies.append(
                pltpu.make_async_remote_copy(
                    src_ref=cut(ref, kv_width, to),
                    dst_ref=dst.at[:, own_key_rows],
                    send_sem=kv_send.at[which, offset],
                    recv_sem=kv_recv.at[which, offset],
                    device_id=(c, to),
                    device_id_type=MESH,
                )
            )
            kv_copies[-1].start()
    for offset in ORDER[1:]:
        to = peer(offset, 1)
        q_copies[offset] = pltpu.make_async_remote_copy(
            src_ref=cut(q_hbm, width, to),
            dst_ref=q_all.at[:, own_rows],
            send_sem=q_send.at[offset],
            recv_sem=q_recv.at[offset],
            device_id=(c, to),
            device_id_type=MESH,
        )
        q_copies[offset].start()

    for copy in small:
        copy.wait()
    upper = []
    for s in range(held):
        block_id = slot_buf[c * held + s]
        upper.append(jnp.where(block_id >= n_cp, 1, 0))
        named = jnp.int32(0)
        for entry in range(LIST):
            named = named + jnp.where(list_buf[s, entry] >= 0, tokens, 0)
        row = jnp.maximum(start_buf[s : s + 1, :] - block_id * tokens, -named)
        for at in range(0, tokens, 128):
            low_bound[s, at : at + 128, :] = jnp.broadcast_to(
                row[:, at : at + 128], (128, 128)
            ).T

    own[1].wait()
    own[2].wait()
    for copy in kv_copies:
        copy.wait_recv()
    for place in range(held):
        slot = (upper[0] + place) % held
        stage[place, 0] = k_all[slot, pl.ds(LIST * tokens, tokens), :]
        stage[place, 1] = v_all[slot, pl.ds(LIST * tokens, tokens), :]

    def far(place, box, side, step):
        return pltpu.make_async_remote_copy(
            src_ref=stage.at[place],
            dst_ref=inbox.at[box],
            send_sem=far_send.at[box],
            recv_sem=far_recv.at[box],
            device_id=(c + side * step, t),
            device_id_type=MESH,
        )

    for step in (1, 2):

        @pl.when(c + step < n_cp)
        def _():
            far(0, step - 1, 1, step).start()

        @pl.when(c >= step)
        def _():
            far(1, step + 1, -1, step).start()

        @pl.when(c < step)
        def _():
            inbox[step - 1] = jnp.zeros(inbox.shape[1:], inbox.dtype)

    @pl.when(c == n_cp - 1)
    def _():
        far(0, 3, -1, 1).start()
        inbox[2] = stage[0]

    for step in (1, 2):

        @pl.when(c >= step)
        def _():
            far(0, step - 1, 1, step).wait_recv()

    @pl.when(c < n_cp - 1)
    def _():
        far(1, 2, -1, 1).wait_recv()
        far(1, 3, -1, 2).wait_recv()

    @pl.when(c == n_cp - 1)
    def _():
        inbox[3] = inbox[0]

    for s in range(held):
        for step in (1, 2):
            box = upper[s] * 2 + step - 1
            rows = pl.ds((LIST - step) * tokens, tokens)
            k_all[s, rows, :] = inbox[box, 0]
            v_all[s, rows, :] = inbox[box, 1]

    lane = lax.broadcasted_iota(jnp.int32, (part, 128), 1)
    sub = lax.broadcasted_iota(jnp.int32, (part, 128), 0)

    def attend(s, source):
        rows = pl.ds(pl.multiple_of(source * part, part), part)
        first = (source // (n_tp // 2)) * (tokens // 2)
        keys = pl.ds(pl.multiple_of(first, tokens // 2), window)
        query = q_all[s, rows, :]
        query = jnp.concatenate(
            [query[:, h * HEAD_SIZE : (h + 1) * HEAD_SIZE] for h in range(group)], axis=0
        )
        scores = lax.dot_general(
            query, k_all[s, keys, :], (((1,), (1,)), ((), ())), preferred_element_type=jnp.float32
        )
        lowest = low_bound[s, rows, :]
        highest = sub + source * part
        visible = []
        for at in range(0, window, 128):
            key = lane + (first + at - LIST * tokens)
            visible.append((key >= lowest) & (key <= highest))
        visible = jnp.concatenate(visible, axis=1)
        scores = scores.reshape(group, part, window)
        scores = jnp.where(visible[None], scores, neg_large)
        scores = scores.reshape(group * part, window)
        best = jnp.max(scores, axis=-1, keepdims=True)
        weights = jnp.exp2((scores - best) * SCALE)
        total = jnp.sum(weights, axis=-1, keepdims=True)
        mixed = jnp.dot(
            weights.astype(jnp.bfloat16), v_all[s, keys, :], preferred_element_type=jnp.float32
        )
        mixed = (mixed * (1.0 / total)).astype(jnp.bfloat16)
        for h in range(group):
            out_buf[s, rows, h * HEAD_SIZE : (h + 1) * HEAD_SIZE] = mixed[
                h * part : (h + 1) * part
            ]

    out_copies = []
    for offset in ORDER:
        if offset == 0:
            own[0].wait()
        else:
            q_copies[offset].wait_recv()
        source = peer(offset, -1)
        for s in range(held):
            attend(s, source)
        rows = pl.ds(pl.multiple_of(source * part, part), part)
        copy = pltpu.make_async_copy(
            out_buf.at[:, rows], out_hbm.at[:, rows], out_sem.at[offset]
        )
        copy.start()
        out_copies.append(copy)

    for copy in kv_copies:
        copy.wait_send()
    for copy in q_copies.values():
        copy.wait_send()
    for step in (1, 2):

        @pl.when(c + step < n_cp)
        def _():
            far(0, step - 1, 1, step).wait_send()

        @pl.when(c >= step)
        def _():
            far(1, step + 1, -1, step).wait_send()

    @pl.when(c == n_cp - 1)
    def _():
        far(0, 3, -1, 1).wait_send()

    for copy in out_copies:
        copy.wait()


def on_device(n_cp, n_tp, query_rows, key_rows, value_matrix, doc_start, source_lists, slot_block):
    held, part, all_width = query_rows.shape
    tokens = part * n_tp
    width = all_width // n_tp
    kv_width = key_rows.shape[2] // n_tp
    reach = (LIST + 1) * tokens
    bf16, i32 = jnp.bfloat16, jnp.int32
    dma = pltpu.SemaphoreType.DMA
    return pl.pallas_call(
        functools.partial(kernel, n_cp, n_tp),
        out_shape=jax.ShapeDtypeStruct((held, tokens, width), bf16),
        in_specs=[pl.BlockSpec(memory_space=pltpu.HBM)] * 6,
        out_specs=pl.BlockSpec(memory_space=pl.ANY),
        scratch_shapes=[
            pltpu.VMEM((held, tokens, width), bf16),
            pltpu.VMEM((held, reach, kv_width), bf16),
            pltpu.VMEM((held, reach, kv_width), bf16),
            pltpu.VMEM((2, 2, tokens, kv_width), bf16),
            pltpu.VMEM((4, 2, tokens, kv_width), bf16),
            pltpu.VMEM((held, tokens, width), bf16),
            pltpu.VMEM((held, tokens), i32),
            pltpu.VMEM((held, tokens, 128), i32),
            pltpu.SMEM(source_lists.shape, i32),
            pltpu.SMEM(slot_block.shape, i32),
            dma((3,)),
            dma((3,)),
            dma((2, n_tp)),
            dma((2, n_tp)),
            dma((n_tp,)),
            dma((n_tp,)),
            dma((4,)),
            dma((4,)),
            dma((n_tp,)),
        ],
        compiler_params=pltpu.CompilerParams(
            collective_id=0, has_side_effects=True, vmem_limit_bytes=40 * 1024 * 1024
        ),
        name="attention",
    )(query_rows, key_rows, value_matrix, doc_start, source_lists, slot_block)


def solution(mesh):
    in_specs = (
        P("cp", "tp", None),
        P("cp", "tp", None),
        P("cp", "tp", None),
        P("cp", None),
        P("cp", None),
        P(),
    )
    out_specs = P("cp", None, "tp")
    return jax.shard_map(
        functools.partial(on_device, mesh.shape["cp"], mesh.shape["tp"]),
        mesh=mesh,
        in_specs=in_specs,
        out_specs=out_specs,
        check_vma=False,
    )
```

time: 127 us -> 40.8 us (0.32)
  the two profiles are of different devices: /device:TPU:254 before, /device:TPU:184 now
where the time goes in v1:
time: 40.8 us; the launch traced here: 40.5 us
  Pallas kernels  34.5 us (85%)
  local copies, waits for them, and re-layouts  6.02 us (15%)
    pallas_call x1, Pallas kernels, on_device(): pl.pallas_call(functools.partial(kernel, n_cp, n_tp), out_shape=jax.Shape...  34.5 us
    unnamed x13, local copies, waits for them, and re-layouts  6.02 us

profile of v1, /device:TPU:184, one launch (start us, length us, event | category | flops | bytes accessed | tf_op | source)
XLA Modules:
  0.0 40.5 jit_solution(10771178875055662661)
XLA Ops:
  0.0 0.0 copy-start
  0.0 1.2 %copy-done = bf16[2,32,8192]{2,1,0:T(8,128)(2,1)S(1)} copy-done((bf16[2,32,8192]{2,1,0:T(8,128)(2,1)S(1)}, bf16[2,32,8192]{2,1,0:T(8,128)(2,1)}, u32[]{:S(2)}) %copy-start) | copy-done | bytes 1048600
  1.2 0.0 copy-start.1
  1.2 0.9 %copy-done.1 = bf16[2,32,1024]{2,1,0:T(8,128)(2,1)S(1)} copy-done((bf16[2,32,1024]{2,1,0:T(8,128)(2,1)S(1)}, bf16[2,32,1024]{2,1,0:T(8,128)(2,1)}, u32[]{:S(2)}) %copy-start.1) | copy-done | bytes 131096
  2.1 0.0 copy-start.2
  2.1 0.9 %copy-done.2 = bf16[2,32,1024]{2,1,0:T(8,128)(2,1)S(1)} copy-done((bf16[2,32,1024]{2,1,0:T(8,128)(2,1)S(1)}, bf16[2,32,1024]{2,1,0:T(8,128)(2,1)}, u32[]{:S(2)}) %copy-start.2) | copy-done | bytes 131096
  3.0 0.0 copy-start.3
  3.0 0.7 %copy-done.3 = s32[2,256]{1,0:T(2,128)S(1)} copy-done((s32[2,256]{1,0:T(2,128)S(1)}, s32[2,256]{1,0:T(2,128)}, u32[]{:S(2)}) %copy-start.3) | copy-done | bytes 2072
  3.7 0.0 copy-start.4
  3.7 0.7 %copy-done.4 = s32[2,2]{1,0:T(2,128)S(1)} copy-done((s32[2,2]{1,0:T(2,128)S(1)}, s32[2,2]{1,0:T(2,128)}, u32[]{:S(2)}) %copy-start.4) | copy-done | bytes 40
  4.4 0.0 copy-start.5
  4.4 0.7 %copy-done.5 = s32[128]{0:T(128)S(1)} copy-done((s32[128]{0:T(128)S(1)}, s32[128]{0:T(128)}, u32[]{:S(2)}) %copy-start.5) | copy-done | bytes 536
  5.1 34.5 %attention.1 = bf16[2,256,1024]{2,1,0:T(8,128)(2,1)S(1)} custom-call(bf16[2,32,8192]{2,1,0:T(8,128)(2,1)S(1)} %copy-done, bf16[2,32,1024]{2,1,0:T(8,128)(2,1)S(1)} %copy-done.1, bf16[2,32,1024]{2,1,0:T(8,128)(2,1)S(1)} %copy-done.2, s32[2,256]{1,0:T(2,128)S(1)} %copy-done.3, s32[2,2]{1,0:T(2,128)S(1)} %copy-done.4, s32[128]{0:T(128)S(1)} %copy-done.5), custom_call_target="tpu_custom_call" | custom-call | tf_op jit(solution)/shard_map/attention/pallas_call | solution.py:289
  39.6 1.0 %copy.8 = bf16[2,256,1024]{2,1,0:T(8,128)(2,1)} copy(bf16[2,256,1024]{2,1,0:T(8,128)(2,1)S(1)} %attention.1) | data formatting | bytes 2097152
Async XLA Ops:
  0.0 1.2 %copy-start = (bf16[2,32,8192]{2,1,0:T(8,128)(2,1)S(1)}, bf16[2,32,8192]{2,1,0:T(8,128)(2,1)}, u32[]{:S(2)}) copy-start(bf16[2,32,8192]{2,1,0:T(8,128)(2,1)} %q_hbm.1) | copy-start | bytes 3145732
  1.2 0.9 %copy-start.1 = (bf16[2,32,1024]{2,1,0:T(8,128)(2,1)S(1)}, bf16[2,32,1024]{2,1,0:T(8,128)(2,1)}, u32[]{:S(2)}) copy-start(bf16[2,32,1024]{2,1,0:T(8,128)(2,1)} %k_hbm.1) | copy-start | bytes 393220
  2.1 0.9 %copy-start.2 = (bf16[2,32,1024]{2,1,0:T(8,128)(2,1)S(1)}, bf16[2,32,1024]{2,1,0:T(8,128)(2,1)}, u32[]{:S(2)}) copy-start(bf16[2,32,1024]{2,1,0:T(8,128)(2,1)} %v_hbm.1) | copy-start | bytes 393220
  3.0 0.7 %copy-start.3 = (s32[2,256]{1,0:T(2,128)S(1)}, s32[2,256]{1,0:T(2,128)}, u32[]{:S(2)}) copy-start(s32[2,256]{1,0:T(2,128)} %start_hbm.1) | copy-start | bytes 6148
  3.7 0.7 %copy-start.4 = (s32[2,2]{1,0:T(2,128)S(1)}, s32[2,2]{1,0:T(2,128)}, u32[]{:S(2)}) copy-start(s32[2,2]{1,0:T(2,128)} %list_hbm.1) | copy-start | bytes 52
  4.4 0.7 %copy-start.5 = (s32[128]{0:T(128)S(1)}, s32[128]{0:T(128)}, u32[]{:S(2)}) copy-start(s32[128]{0:T(128)} %slot_hbm.1) | copy-start | bytes 1540

commit v2 on v1

v2 whole, which is shorter than its diff:
```python
import functools

import jax
import jax.numpy as jnp
from jax import lax
from jax.experimental import pallas as pl
from jax.experimental.pallas import tpu as pltpu
from jax.sharding import PartitionSpec as P

QUERY_HEAD_COUNT = 64
KEY_VALUE_HEADS = 8
HEAD_SIZE = 128
LIST = 2
MESH = pl.DeviceIdType.MESH

neg_large = -1e30
SCALE = HEAD_SIZE ** (-0.5) * 1.4426950408889634
RUN = 2
ORDER = (1, 2, 6, 3, 7, 4, 5)
AHEAD = 3
GROUP = 16
LEGS = (GROUP, 2 - GROUP)


def kernel(
    n_cp,
    n_tp,
    q_hbm,
    k_hbm,
    v_hbm,
    start_hbm,
    list_hbm,
    slot_hbm,
    out_ref,
    q_all,
    k_all,
    v_all,
    stage,
    inbox,
    relay,
    start_buf,
    low_bound,
    list_buf,
    slot_buf,
    small_sem,
    own_sem,
    kv_send,
    kv_recv,
    q_send,
    q_recv,
    far_send,
    far_recv,
    relay_recv,
):
    held, part, _ = q_hbm.shape
    tokens = part * n_tp
    width = q_hbm.shape[2] // n_tp
    kv_width = k_hbm.shape[2] // n_tp
    group = width // HEAD_SIZE
    window = LIST * tokens + tokens // 2
    c = lax.axis_index("cp")
    t = lax.axis_index("tp")
    n_x = n_tp // RUN
    x, z = t // RUN, t % RUN

    def peer(offset, sign):
        dx, dz = offset // RUN, offset % RUN
        return ((x + sign * dx + n_x) % n_x) * RUN + (z + sign * dz + RUN) % RUN

    def climbs(who):
        return (who >= 0) & (who + GROUP < n_cp) & ((who + 2 * GROUP) % GROUP == GROUP - 2)

    def descends(who):
        return (who >= GROUP) & (who < n_cp) & (who % GROUP == 1)

    leg, rest = LEGS
    even = c % 2 == 0
    odd = c % 2 == 1
    relays_low, relays_high = climbs(c - leg), descends(c + leg)

    partners = [
        (c >= 1, -1),
        (c >= 2, -2),
        (c + 1 < n_cp, 1),
        (c + 2 < n_cp, 2),
        (climbs(c), leg),
        (relays_low, -leg),
        (relays_low, rest),
        (climbs(c - leg - rest), -rest),
        (descends(c), -leg),
        (relays_high, leg),
        (relays_high, -rest),
        (descends(c + leg + rest), rest),
    ]
    barrier = pltpu.get_barrier_semaphore()
    for offset in range(1, n_tp):
        pl.semaphore_signal(
            barrier, inc=1, device_id=(c, peer(offset, 1)), device_id_type=MESH
        )
    greeted = n_tp - 1
    for near, distance in partners:
        greeted = greeted + jnp.where(near, 1, 0)

        @pl.when(near)
        def _():
            pl.semaphore_signal(
                barrier, inc=1, device_id=(c + distance, t), device_id_type=MESH
            )

    small = [
        pltpu.make_async_copy(start_hbm, start_buf, small_sem.at[0]),
        pltpu.make_async_copy(list_hbm, list_buf, small_sem.at[1]),
        pltpu.make_async_copy(slot_hbm, slot_buf, small_sem.at[2]),
    ]
    own_rows = pl.ds(pl.multiple_of(t * part, part), part)
    own_key_rows = pl.ds(pl.multiple_of(LIST * tokens + t * part, part), part)

    def cut(ref, size, which):
        return ref.at[:, :, pl.ds(pl.multiple_of(which * size, size), size)]

    own = [
        pltpu.make_async_copy(cut(k_hbm, kv_width, t), k_all.at[:, own_key_rows], own_sem.at[0]),
        pltpu.make_async_copy(cut(v_hbm, kv_width, t), v_all.at[:, own_key_rows], own_sem.at[1]),
        pltpu.make_async_copy(cut(q_hbm, width, t), q_all.at[:, own_rows], own_sem.at[2]),
    ]
    for copy in small + own:
        copy.start()
    pl.semaphore_wait(barrier, greeted)

    kv_copies = ([], [])
    q_copies = {}
    for which, (ref, dst) in enumerate(((k_hbm, k_all), (v_hbm, v_all))):
        for offset in ORDER:
            to = peer(offset, 1)
            copy = pltpu.make_async_remote_copy(
                src_ref=cut(ref, kv_width, to),
                dst_ref=dst.at[:, own_key_rows],
                send_sem=kv_send.at[which, offset],
                recv_sem=kv_recv.at[which, offset],
                device_id=(c, to),
                device_id_type=MESH,
            )
            copy.start()
            kv_copies[which].append(copy)
    for offset in ORDER:
        to = peer(offset, 1)
        q_copies[offset] = pltpu.make_async_remote_copy(
            src_ref=cut(q_hbm, width, to),
            dst_ref=q_all.at[:, own_rows],
            send_sem=q_send.at[offset],
            recv_sem=q_recv.at[offset],
            device_id=(c, to),
            device_id_type=MESH,
        )

    for offset in ORDER[:AHEAD]:
        q_copies[offset].start()

    for copy in small:
        copy.wait()
    upper = []
    for s in range(held):
        block_id = slot_buf[c * held + s]
        upper.append(jnp.where(block_id >= n_cp, 1, 0))
        named = jnp.int32(0)
        for entry in range(LIST):
            named = named + jnp.where(list_buf[s, entry] >= 0, tokens, 0)
        row = jnp.maximum(start_buf[s : s + 1, :] - block_id * tokens, -named)
        for at in range(0, tokens, 128):
            low_bound[s, at : at + 128, :] = jnp.broadcast_to(
                row[:, at : at + 128], (128, 128)
            ).T

    def far(which, src, dst, order, recv, distance):
        return pltpu.make_async_remote_copy(
            src_ref=src.at[which],
            dst_ref=dst.at[which],
            send_sem=far_send.at[order, which],
            recv_sem=recv.at[which],
            device_id=(c + distance, t),
            device_id_type=MESH,
        )

    low, high = stage.at[0], stage.at[1]
    box = [inbox.at[i] for i in range(4)]
    box_recv = [far_recv.at[i] for i in range(4)]
    first = [
        (c + 1 < n_cp, low, box[0], box_recv[0], 1),
        (c >= 1, high, box[2], box_recv[2], -1),
        (even & (c + 2 < n_cp) & ~climbs(c), low, box[1], box_recv[1], 2),
        (odd & (c >= 2) & ~descends(c), high, box[3], box_recv[3], -2),
        (climbs(c), low, relay, relay_recv, leg),
        (descends(c), high, relay, relay_recv, -leg),
    ]
    then = [
        (even & (c >= 2), box[0], box[1], box_recv[1], 1),
        (odd, box[2], box[3], box_recv[3], -1),
        (relays_low, relay, box[1], box_recv[1], rest),
        (relays_high, relay, box[3], box_recv[3], -rest),
    ]
    moves = [(order,) + move for order, move in enumerate(first + then)]

    def send(move, which):
        order, when, src, dst, recv, distance = move

        @pl.when(when)
        def _():
            far(which, src, dst, order, recv, distance).start()

    def arrive(when, which, dst, recv):
        @pl.when(when)
        def _():
            far(which, dst, dst, 0, recv, 0).wait_recv()

    for which, whole in enumerate((k_all, v_all)):
        own[which].wait()
        for copy in kv_copies[which]:
            copy.wait_recv()
        for place in range(held):
            slot = (upper[0] + place) % held
            stage[place, which] = whole[slot, pl.ds(LIST * tokens, tokens), :]
        for move in moves[: len(first)]:
            send(move, which)

    for offset in ORDER[AHEAD:]:
        q_copies[offset].start()

    @pl.when(c < 1)
    def _():
        inbox[0] = jnp.zeros(inbox.shape[1:], inbox.dtype)

    @pl.when(c < 2)
    def _():
        inbox[1] = jnp.zeros(inbox.shape[1:], inbox.dtype)

    @pl.when(c == n_cp - 1)
    def _():
        inbox[2] = stage[0]

    for which in range(2):
        arrive(even & (c >= 2), which, box[0], box_recv[0])
        arrive(odd & (c < n_cp - 1), which, box[2], box_recv[2])
        for move in moves[len(first) : len(first) + 2]:
            send(move, which)
        arrive(relays_low | relays_high, which, relay, relay_recv)
        for move in moves[len(first) + 2 :]:
            send(move, which)
    for which in range(2):
        arrive(odd, which, box[0], box_recv[0])
        arrive(c >= 2, which, box[1], box_recv[1])
        arrive(even, which, box[2], box_recv[2])
        arrive(c < n_cp - 1, which, box[3], box_recv[3])

    @pl.when(c == n_cp - 1)
    def _():
        inbox[3] = inbox[0]

    for s in range(held):
        for step in range(LIST):
            source = upper[s] * 2 + step
            rows = pl.ds((LIST - 1 - step) * tokens, tokens)
            k_all[s, rows, :] = inbox[source, 0]
            v_all[s, rows, :] = inbox[source, 1]

    def attend(s, start, size, half):
        rows = pl.ds(pl.multiple_of(start, size), size)
        begin = half * (tokens // 2)
        keys = pl.ds(pl.multiple_of(begin, tokens // 2), window)
        lane = lax.broadcasted_iota(jnp.int32, (size, 128), 1)
        sub = lax.broadcasted_iota(jnp.int32, (size, 128), 0)
        query = q_all[s, rows, :]
        query = jnp.concatenate(
            [query[:, h * HEAD_SIZE : (h + 1) * HEAD_SIZE] for h in range(group)], axis=0
        )
        scores = lax.dot_general(
            query, k_all[s, keys, :], (((1,), (1,)), ((), ())), preferred_element_type=jnp.float32
        )
        lowest = low_bound[s, rows, :]
        highest = sub + start
        visible = []
        for at in range(0, window, 128):
            key = lane + (begin + at - LIST * tokens)
            visible.append((key >= lowest) & (key <= highest))
        visible = jnp.concatenate(visible, axis=1)
        scores = scores.reshape(group, size, window)
        scores = jnp.where(visible[None], scores, neg_large)
        scores = scores.reshape(group * size, window)
        best = jnp.max(scores, axis=-1, keepdims=True)
        weights = jnp.exp2((scores - best) * SCALE)
        total = jnp.sum(weights, axis=-1, keepdims=True)
        mixed = jnp.dot(
            weights.astype(jnp.bfloat16), v_all[s, keys, :], preferred_element_type=jnp.float32
        )
        mixed = (mixed * (1.0 / total)).astype(jnp.bfloat16)
        for h in range(group):
            out_ref[s, rows, h * HEAD_SIZE : (h + 1) * HEAD_SIZE] = mixed[
                h * size : (h + 1) * size
            ]

    own[2].wait()
    for offsets in ((0, 1), (2, 3), (6, 7), (4,), (5,)):
        for offset in offsets:
            if offset:
                q_copies[offset].wait_recv()
        source_x = (x - offsets[0] // RUN + n_x) % n_x
        source = source_x * RUN if len(offsets) == RUN else peer(offsets[0], -1)
        for s in range(held):
            attend(s, source * part, len(offsets) * part, source_x // (n_x // 2))

    for copy in kv_copies[0] + kv_copies[1] + list(q_copies.values()):
        copy.wait_send()
    for order, when, src, dst, recv, distance in moves:

        @pl.when(when)
        def _():
            for which in range(2):
                far(which, src, dst, order, recv, distance).wait_send()


def on_device(n_cp, n_tp, *operands):
    query_rows, key_rows, _, _, source_lists, slot_block = operands
    held, part, all_width = query_rows.shape
    tokens = part * n_tp
    width = all_width // n_tp
    kv_width = key_rows.shape[2] // n_tp
    reach = (LIST + 1) * tokens
    bf16, i32 = jnp.bfloat16, jnp.int32
    dma = pltpu.SemaphoreType.DMA
    return pl.pallas_call(
        functools.partial(kernel, n_cp, n_tp),
        out_shape=pltpu.VMEM((held, tokens, width), bf16),
        in_specs=[pl.BlockSpec(memory_space=pltpu.HBM)] * 6,
        out_specs=pl.BlockSpec(memory_space=pltpu.VMEM),
        scratch_shapes=[
            pltpu.VMEM((held, tokens, width), bf16),
            pltpu.VMEM((held, reach, kv_width), bf16),
            pltpu.VMEM((held, reach, kv_width), bf16),
            pltpu.VMEM((2, 2, tokens, kv_width), bf16),
            pltpu.VMEM((4, 2, tokens, kv_width), bf16),
            pltpu.VMEM((2, tokens, kv_width), bf16),
            pltpu.VMEM((held, tokens), i32),
            pltpu.VMEM((held, tokens, 128), i32),
            pltpu.SMEM(source_lists.shape, i32),
            pltpu.SMEM(slot_block.shape, i32),
            dma((3,)),
            dma((3,)),
            dma((2, n_tp)),
            dma((2, n_tp)),
            dma((n_tp,)),
            dma((n_tp,)),
            dma((10, 2)),
            dma((4, 2)),
            dma((2,)),
        ],
        compiler_params=pltpu.CompilerParams(
            collective_id=0, has_side_effects=True, vmem_limit_bytes=40 * 1024 * 1024
        ),
        name="attention",
    )(*(pltpu.with_memory_space_constraint(operand, pltpu.HBM) for operand in operands))


def solution(mesh):
    in_specs = (
        P("cp", "tp", None),
        P("cp", "tp", None),
        P("cp", "tp", None),
        P("cp", None),
        P("cp", None),
        P(),
    )
    out_specs = P("cp", None, "tp")
    return jax.shard_map(
        functools.partial(on_device, mesh.shape["cp"], mesh.shape["tp"]),
        mesh=mesh,
        in_specs=in_specs,
        out_specs=out_specs,
        check_vma=False,
    )
```

time: 40.8 us -> 32.1 us (0.79)
  the two profiles are of different devices: /device:TPU:184 before, /device:TPU:256 now
where the time goes in v2:
time: 32.1 us; the launch traced here: 32 us
  Pallas kernels  31 us (97%)
  local copies, waits for them, and re-layouts  0.97 us (3%)
    pallas_call x1, Pallas kernels, on_device(): pl.pallas_call(functools.partial(kernel, n_cp, n_tp), out_shape=pltpu.VME...  31 us
    unnamed x1, local copies, waits for them, and re-layouts  0.97 us

profile of v2, /device:TPU:256, one launch (start us, length us, event | category | flops | bytes accessed | tf_op | source)
XLA Modules:
  0.0 32.0 jit_solution(14303238126070491453)
XLA Ops:
  0.0 31.0 %attention.1 = bf16[2,256,1024]{2,1,0:T(8,128)(2,1)S(1)} custom-call(bf16[2,32,8192]{2,1,0:T(8,128)(2,1)} %q_hbm.1, bf16[2,32,1024]{2,1,0:T(8,128)(2,1)} %k_hbm.1, bf16[2,32,1024]{2,1,0:T(8,128)(2,1)} %v_hbm.1, s32[2,256]{1,0:T(2,128)} %start_hbm.1, s32[2,2]{1,0:T(2,128)} %list_hbm.1, s32[128]{0:T(128)} %slot_hbm.1), custom_call_target="tpu_custom_call" | custom-call | tf_op jit(solution)/shard_map/attention/pallas_call | solution.py:329
  31.0 1.0 %copy.8 = bf16[2,256,1024]{2,1,0:T(8,128)(2,1)} copy(bf16[2,256,1024]{2,1,0:T(8,128)(2,1)S(1)} %attention.1) | data formatting | bytes 2097152

commit v3 on v2

v3 whole, which is shorter than its diff:
```python
import functools

import jax
import jax.numpy as jnp
from jax import lax
from jax.experimental import pallas as pl
from jax.experimental.pallas import tpu as pltpu
from jax.sharding import PartitionSpec as P

QUERY_HEAD_COUNT = 64
KEY_VALUE_HEADS = 8
HEAD_SIZE = 128
LIST = 2
MESH = pl.DeviceIdType.MESH

neg_large = -1e30
SCALE = HEAD_SIZE ** (-0.5) * 1.4426950408889634
RUN = 2
ORDER = (1, 2, 6, 3, 7, 4, 5)
AHEAD = 3
SCHEDULE = (
    ("a", (0, 1)),
    ("a", (2, 3)),
    ("hand", ()),
    ("a", (6, 7)),
    ("keys", ()),
    ("b", (0, 1)),
    ("b", (2, 3)),
    ("b", (6, 7)),
    ("a", (4,)),
    ("b", (4,)),
    ("a", (5,)),
    ("b", (5,)),
)
GROUP = 16
ASIDE = ((14, 0, 16, -14), (14, 1, 14, -12), (15, 1, 3, -2))


def kernel(
    n_cp,
    n_tp,
    q_hbm,
    k_hbm,
    v_hbm,
    start_hbm,
    list_hbm,
    slot_hbm,
    out_ref,
    q_all,
    k_all,
    v_all,
    k_raw,
    v_raw,
    k_cut,
    v_cut,
    relay,
    done,
    start_buf,
    low_bound,
    list_buf,
    slot_buf,
    small_sem,
    raw_sem,
    own_sem,
    kv_send,
    kv_recv,
    q_send,
    q_recv,
    far_send,
    far_recv,
    relay_recv,
    answer,
):
    held, part, _ = q_hbm.shape
    tokens = part * n_tp
    width = q_hbm.shape[2] // n_tp
    kv_width = k_hbm.shape[2] // n_tp
    group = width // HEAD_SIZE
    window = LIST * tokens + tokens // 2
    c = lax.axis_index("cp")
    t = lax.axis_index("tp")
    n_x = n_tp // RUN
    x, z = t // RUN, t % RUN

    def peer(offset, sign):
        dx, dz = offset // RUN, offset % RUN
        return ((x + sign * dx + n_x) % n_x) * RUN + (z + sign * dz + RUN) % RUN

    def climbs(who, place):
        return (who >= 0) & (who + GROUP < n_cp) & ((who + 2 * GROUP) % GROUP == place)

    def descends(who, place):
        return (who >= GROUP) & (who < n_cp) & (who % GROUP == GROUP - 1 - place)

    even = c % 2 == 0
    odd = c % 2 == 1

    pairs = []

    def pair(holds, distance):
        if distance > 0:
            pairs.append((holds(c), holds(c - distance), distance, True))
        else:
            pairs.append((holds(c - distance), holds(c), -distance, False))
        return len(pairs) - 1

    near = [pair(lambda who, d=d: (who >= 0) & (who + d < n_cp), d) for d in (1, 2)]
    outward, onward = {}, {}
    for place, which, leg, rest in ASIDE:
        for goes, way in ((climbs, 1), (descends, -1)):
            go = functools.partial(goes, place=place)
            outward[place, which, way] = pair(go, way * leg)
            onward[place, which, way] = pair(lambda who, go=go, leg=way * leg: go(who - leg), way * rest)

    barrier = pltpu.get_barrier_semaphore()
    for offset in range(1, n_tp):
        pl.semaphore_signal(
            barrier, inc=1, device_id=(c, peer(offset, 1)), device_id_type=MESH
        )
    greeted = n_tp - 1
    for is_lower, is_upper, distance, _ in pairs:
        greeted = greeted + jnp.where(is_upper, 1, 0)

        @pl.when(is_lower)
        def _():
            pl.semaphore_signal(
                barrier, inc=1, device_id=(c + distance, t), device_id_type=MESH
            )

    def answered(number):
        @pl.when(pairs[number][0])
        def _():
            pl.semaphore_wait(answer.at[number], 1)

    small = [
        pltpu.make_async_copy(slot_hbm, slot_buf, small_sem.at[0]),
        pltpu.make_async_copy(start_hbm, start_buf, small_sem.at[1]),
        pltpu.make_async_copy(list_hbm, list_buf, small_sem.at[2]),
    ]
    raw = [
        pltpu.make_async_copy(k_hbm, k_raw, raw_sem.at[0]),
        pltpu.make_async_copy(v_hbm, v_raw, raw_sem.at[1]),
    ]
    own_rows = pl.ds(pl.multiple_of(t * part, part), part)
    own_key_rows = pl.ds(pl.multiple_of(LIST * tokens + t * part, part), part)

    def cut(ref, size, which):
        return ref.at[:, :, pl.ds(pl.multiple_of(which * size, size), size)]

    own = [
        pltpu.make_async_copy(cut(k_cut, kv_width, t), k_all.at[:, own_key_rows], own_sem.at[0]),
        pltpu.make_async_copy(cut(v_cut, kv_width, t), v_all.at[:, own_key_rows], own_sem.at[1]),
        pltpu.make_async_copy(cut(q_hbm, width, t), q_all.at[:, own_rows], own_sem.at[2]),
    ]
    for copy in small[:1] + raw + small[1:] + own[2:]:
        copy.start()

    small[0].wait()
    block_ids = [slot_buf[c * held + s] for s in range(held)]
    swapped = block_ids[0] >= n_cp

    def in_place(place, of_slot):
        return jnp.where(swapped, of_slot(1 - place), of_slot(place))

    for which, (ref, dst) in enumerate(((k_raw, k_cut), (v_raw, v_cut))):
        raw[which].wait()
        for place in range(held):
            dst[place] = in_place(place, lambda s: ref[s])
        own[which].start()
    pl.semaphore_wait(barrier, greeted)

    kv_copies = ([], [])
    q_copies = {}
    for which, (ref, dst) in enumerate(((k_cut, k_all), (v_cut, v_all))):
        for offset in ORDER:
            to = peer(offset, 1)
            copy = pltpu.make_async_remote_copy(
                src_ref=cut(ref, kv_width, to),
                dst_ref=dst.at[:, own_key_rows],
                send_sem=kv_send.at[which, offset],
                recv_sem=kv_recv.at[which, offset],
                device_id=(c, to),
                device_id_type=MESH,
            )
            copy.start()
            kv_copies[which].append(copy)
    for offset in ORDER:
        to = peer(offset, 1)
        q_copies[offset] = pltpu.make_async_remote_copy(
            src_ref=cut(q_hbm, width, to),
            dst_ref=q_all.at[:, own_rows],
            send_sem=q_send.at[offset],
            recv_sem=q_recv.at[offset],
            device_id=(c, to),
            device_id_type=MESH,
        )
    for offset in ORDER[:AHEAD]:
        q_copies[offset].start()

    for number, (is_lower, is_upper, distance, sends) in enumerate(pairs):

        @pl.when(is_upper & sends)
        def _():
            pl.semaphore_signal(
                answer.at[number], inc=1, device_id=(c - distance, t), device_id_type=MESH
            )

    for copy in small[1:]:
        copy.wait()

    def lowest_of(s):
        named = jnp.int32(0)
        for entry in range(LIST):
            named = named + jnp.where(list_buf[s, entry] >= 0, tokens, 0)
        return jnp.maximum(start_buf[s : s + 1, :] - block_ids[s] * tokens, -named)

    for place in range(held):
        row = in_place(place, lowest_of)
        for at in range(0, tokens, 128):
            low_bound[place, at : at + 128, :] = jnp.broadcast_to(
                row[:, at : at + 128], (128, 128)
            ).T

    def segment(place, below):
        rows = pl.ds((LIST - below) * tokens, tokens)
        return [k_all.at[place, rows], v_all.at[place, rows]]

    def far(which, src, dst, order, recv, distance):
        return pltpu.make_async_remote_copy(
            src_ref=src[which],
            dst_ref=dst[which],
            send_sem=far_send.at[order, which],
            recv_sem=recv[which],
            device_id=(c + distance, t),
            device_id_type=MESH,
        )

    low, high = segment(0, 0), segment(1, 0)
    low_1, low_2, high_1, high_2 = segment(0, 1), segment(0, 2), segment(1, 1), segment(1, 2)
    low_1_in, low_2_in, high_1_in, high_2_in = [
        [far_recv.at[i, which] for which in range(2)] for i in range(4)
    ]
    aside, aside_in = [relay.at[0], relay.at[1]], [relay_recv.at[0], relay_recv.at[1]]
    last = c == n_cp - 1
    late = (c % GROUP == 0) | ((c % GROUP == GROUP - 1) & ~last)
    hand_low, hand_high = even & (c >= 2), odd
    both, edge = (0, 1), GROUP - 1
    first = [
        ((0,), c + 1 < n_cp, low, low_1, low_1_in, 1),
        ((1,), (c + 1 < n_cp) & ~climbs(c, edge), low, low_1, low_1_in, 1),
        ((0,), c >= 1, high, high_1, high_1_in, -1),
        ((1,), (c >= 1) & ~descends(c, edge), high, high_1, high_1_in, -1),
        (both, even & (c + 2 < n_cp) & ~climbs(c, edge - 1), low, low_2, low_2_in, 2),
        (both, odd & (c >= 2) & ~descends(c, edge - 1), high, high_2, high_2_in, -2),
    ]
    passed = []
    for place, which, leg, rest in ASIDE:
        first += [
            ((which,), climbs(c, place), low, aside, aside_in, leg),
            ((which,), descends(c, place), high, aside, aside_in, -leg),
        ]
        to_low, to_high = (low_1, high_1) if place == edge else (low_2, high_2)
        in_low, in_high = (low_1_in, high_1_in) if place == edge else (low_2_in, high_2_in)
        passed += [
            ((which,), climbs(c - leg, place), aside, to_low, in_low, rest),
            ((which,), descends(c + leg, place), aside, to_high, in_high, -rest),
        ]
    handed = [
        (both, hand_low, low_1, low_2, low_2_in, 1),
        (both, hand_high, high_1, high_2, high_2_in, -1),
    ]
    moves = [(order,) + move for order, move in enumerate(first + passed + handed)]
    ways = [key + (way,) for key in ((a[0], a[1]) for a in ASIDE) for way in (1, -1)]
    waits = {len(first) - len(ways) + i: outward[key] for i, key in enumerate(ways)}
    waits.update({len(first) + i: onward[key] for i, key in enumerate(ways)})
    first, passed, handed = moves[: len(first)], moves[len(first) : -2], moves[-2:]

    def send(move, which, also=True):
        order, whiches, when, src, dst, recv, distance = move
        if which in whiches:
            if order in waits and distance > 0:
                answered(waits[order])

            @pl.when(when & also)
            def _():
                far(which, src, dst, order, recv, distance).start()

    def arrive(when, which, dst, recv):
        @pl.when(when)
        def _():
            far(which, dst, dst, 0, recv, 0).wait_recv()

    def hand_on(which, also):
        arrive(hand_low & also, which, low_1, low_1_in)
        arrive(hand_high & ~last & also, which, high_1, high_1_in)
        for move in handed:
            send(move, which, also)

    for which in range(2):
        own[which].wait()
        for copy in kv_copies[which]:
            copy.wait_recv()
        for move in first:
            if move[-1] < 0:
                send(move, which)
        if which == 0:
            for number in near:
                answered(number)
        for move in first:
            if move[-1] > 0:
                send(move, which)
    for offset in ORDER[AHEAD:]:
        q_copies[offset].start()

    for which in range(2):

        @pl.when(c < 1)
        def _():
            low_1[which][...] = jnp.zeros((tokens, kv_width), k_all.dtype)

        @pl.when(c < 2)
        def _():
            low_2[which][...] = jnp.zeros((tokens, kv_width), k_all.dtype)

        @pl.when(last)
        def _():
            high_1[which][...] = low[which][...]

    for which in range(2):
        hand_on(which, ~late)
        for move in passed:
            if which in move[1]:
                arrive(move[2], which, aside, aside_in)
            send(move, which)

    place_a = jnp.where(c % GROUP < 2, 1, 0)
    place_b = 1 - place_a

    def keys_in(place):
        for which in range(2):
            arrive((place == 0) & odd, which, low_1, low_1_in)
            arrive((place == 0) & (c >= 2), which, low_2, low_2_in)
            arrive((place == 1) & even, which, high_1, high_1_in)
            arrive((place == 1) & ~last, which, high_2, high_2_in)

            @pl.when((place == 1) & last)
            def _():
                high_2[which][...] = low_1[which][...]

    def attend(place, start, size, half):
        rows = pl.ds(pl.multiple_of(start, size), size)
        slot = jnp.where(swapped, 1 - place, place)
        begin = half * (tokens // 2)
        keys = pl.ds(pl.multiple_of(begin, tokens // 2), window)
        lane = lax.broadcasted_iota(jnp.int32, (size, 128), 1)
        sub = lax.broadcasted_iota(jnp.int32, (size, 128), 0)
        query = jnp.where(slot == 0, q_all[0, rows, :], q_all[1, rows, :])
        query = jnp.concatenate(
            [query[:, h * HEAD_SIZE : (h + 1) * HEAD_SIZE] for h in range(group)], axis=0
        )
        scores = lax.dot_general(
            query, k_all[place, keys, :], (((1,), (1,)), ((), ())), preferred_element_type=jnp.float32
        )
        lowest = low_bound[place, rows, :]
        highest = sub + start
        visible = []
        for at in range(0, window, 128):
            key = lane + (begin + at - LIST * tokens)
            visible.append((key >= lowest) & (key <= highest))
        visible = jnp.concatenate(visible, axis=1)
        scores = scores.reshape(group, size, window)
        scores = jnp.where(visible[None], scores, neg_large)
        scores = scores.reshape(group * size, window)
        best = jnp.max(scores, axis=-1, keepdims=True)
        weights = jnp.exp2((scores - best) * SCALE)
        total = jnp.sum(weights, axis=-1, keepdims=True)
        mixed = jnp.dot(
            weights.astype(jnp.bfloat16), v_all[place, keys, :], preferred_element_type=jnp.float32
        )
        mixed = (mixed * (1.0 / total)).astype(jnp.bfloat16)
        return jnp.concatenate([mixed[h * size : (h + 1) * size] for h in range(group)], axis=1)

    def part_of(offsets):
        source_x = (x - offsets[0] // RUN + n_x) % n_x
        source = source_x * RUN if len(offsets) == RUN else peer(offsets[0], -1)
        return source * part, len(offsets) * part, source_x // (n_x // 2)

    own[2].wait()
    keys_in(place_a)
    arrived = {0}
    for turn, offsets in SCHEDULE:
        if turn == "hand":
            for which in range(2):
                hand_on(which, late)
            continue
        if turn == "keys":
            keys_in(place_b)
            continue
        for offset in offsets:
            if offset not in arrived:
                arrived.add(offset)
                q_copies[offset].wait_recv()
        start, size, half = part_of(offsets)
        rows = pl.ds(pl.multiple_of(start, size), size)
        if turn == "a":
            done[rows, :] = attend(place_a, start, size, half)
        else:
            result_a, result_b = done[rows, :], attend(place_b, start, size, half)
            b_is_0 = swapped == (place_b == 1)
            out_ref[0, rows, :] = jnp.where(b_is_0, result_b, result_a)
            out_ref[1, rows, :] = jnp.where(b_is_0, result_a, result_b)

    for copy in kv_copies[0] + kv_copies[1] + list(q_copies.values()):
        copy.wait_send()
    for order, whiches, when, src, dst, recv, distance in moves:

        @pl.when(when)
        def _():
            for which in whiches:
                far(which, src, dst, order, recv, distance).wait_send()


def on_device(n_cp, n_tp, *operands):
    query_rows, key_rows, _, _, source_lists, slot_block = operands
    held, part, all_width = query_rows.shape
    tokens = part * n_tp
    width = all_width // n_tp
    kv_width = key_rows.shape[2] // n_tp
    reach = (LIST + 1) * tokens
    bf16, i32 = jnp.bfloat16, jnp.int32
    dma = pltpu.SemaphoreType.DMA
    return pl.pallas_call(
        functools.partial(kernel, n_cp, n_tp),
        out_shape=pltpu.VMEM((held, tokens, width), bf16),
        in_specs=[pl.BlockSpec(memory_space=pltpu.HBM)] * 6,
        out_specs=pl.BlockSpec(memory_space=pltpu.VMEM),
        scratch_shapes=[
            pltpu.VMEM((held, tokens, width), bf16),
            pltpu.VMEM((held, reach, kv_width), bf16),
            pltpu.VMEM((held, reach, kv_width), bf16),
            pltpu.VMEM(key_rows.shape, bf16),
            pltpu.VMEM(key_rows.shape, bf16),
            pltpu.VMEM(key_rows.shape, bf16),
            pltpu.VMEM(key_rows.shape, bf16),
            pltpu.VMEM((2, tokens, kv_width), bf16),
            pltpu.VMEM((tokens, width), bf16),
            pltpu.VMEM((held, tokens), i32),
            pltpu.VMEM((held, tokens, 128), i32),
            pltpu.SMEM(source_lists.shape, i32),
            pltpu.SMEM(slot_block.shape, i32),
            dma((3,)),
            dma((2,)),
            dma((3,)),
            dma((2, n_tp)),
            dma((2, n_tp)),
            dma((n_tp,)),
            dma((n_tp,)),
            dma((8 + 4 * len(ASIDE), 2)),
            dma((4, 2)),
            dma((2,)),
            pltpu.SemaphoreType.REGULAR((2 + 4 * len(ASIDE),)),
        ],
        compiler_params=pltpu.CompilerParams(
            collective_id=0, has_side_effects=True, vmem_limit_bytes=40 * 1024 * 1024
        ),
        name="attention",
    )(*(pltpu.with_memory_space_constraint(operand, pltpu.HBM) for operand in operands))


def solution(mesh):
    in_specs = (
        P("cp", "tp", None),
        P("cp", "tp", None),
        P("cp", "tp", None),
        P("cp", None),
        P("cp", None),
        P(),
    )
    out_specs = P("cp", None, "tp")
    return jax.shard_map(
        functools.partial(on_device, mesh.shape["cp"], mesh.shape["tp"]),
        mesh=mesh,
        in_specs=in_specs,
        out_specs=out_specs,
        check_vma=False,
    )
```

time: 32.1 us -> 29.1 us (0.907)
  the two profiles are of different devices: /device:TPU:256 before, /device:TPU:184 now
where the time goes in v3:
time: 29.1 us; the launch traced here: 28.7 us
  Pallas kernels  27.7 us (95%)
  local copies, waits for them, and re-layouts  0.97 us (3%)
    pallas_call x1, Pallas kernels, on_device(): pl.pallas_call(functools.partial(kernel, n_cp, n_tp), out_shape=pltpu.VME...  27.7 us
    unnamed x1, local copies, waits for them, and re-layouts  0.97 us

profile of v3, /device:TPU:184, one launch (start us, length us, event | category | flops | bytes accessed | tf_op | source)
XLA Modules:
  0.0 28.7 jit_solution(16527142196762084008)
XLA Ops:
  0.0 27.7 %attention.1 = bf16[2,256,1024]{2,1,0:T(8,128)(2,1)S(1)} custom-call(bf16[2,32,8192]{2,1,0:T(8,128)(2,1)} %q_hbm.1, bf16[2,32,1024]{2,1,0:T(8,128)(2,1)} %k_hbm.1, bf16[2,32,1024]{2,1,0:T(8,128)(2,1)} %v_hbm.1, s32[2,256]{1,0:T(2,128)} %start_hbm.1, s32[2,2]{1,0:T(2,128)} %list_hbm.1, s32[128]{0:T(128)} %slot_hbm.1), custom_call_target="tpu_custom_call" | custom-call | tf_op jit(solution)/shard_map/attention/pallas_call | solution.py:432
  27.7 1.0 %copy.8 = bf16[2,256,1024]{2,1,0:T(8,128)(2,1)} copy(bf16[2,256,1024]{2,1,0:T(8,128)(2,1)S(1)} %attention.1) | data formatting | bytes 2097152

commit v4 on v3

--- a/solution.py
+++ b/solution.py
@@ -19,21 +19,15 @@
 ORDER = (1, 2, 6, 3, 7, 4, 5)
 AHEAD = 3
 SCHEDULE = (
-    ("a", (0, 1)),
-    ("a", (2, 3)),
-    ("hand", ()),
-    ("a", (6, 7)),
-    ("keys", ()),
-    ("b", (0, 1)),
-    ("b", (2, 3)),
-    ("b", (6, 7)),
-    ("a", (4,)),
-    ("b", (4,)),
-    ("a", (5,)),
-    ("b", (5,)),
+    (("a", (0, 1)), ("a", (2, 3))),
+    "keys",
+    (("b", (0, 1)), ("b", (2, 3))),
+    (("a", (6, 7)), ("b", (6, 7))),
+    (("a", (4,)), ("b", (4,))),
+    (("a", (5,)), ("b", (5,))),
 )
 GROUP = 16
-ASIDE = ((14, 0, 16, -14), (14, 1, 14, -12), (15, 1, 3, -2))
+ASIDE = ((14, 0, 16, -14), (14, 1, 14, -12), (15, 0, 1, 0), (15, 1, 3, -2))
 
 
 def kernel(
@@ -69,6 +63,7 @@
     far_send,
     far_recv,
     relay_recv,
+    cross_send,
     answer,
 ):
     held, part, _ = q_hbm.shape
@@ -97,11 +92,11 @@
 
     pairs = []
 
-    def pair(holds, distance):
+    def pair(holds, distance, whole=False):
         if distance > 0:
-            pairs.append((holds(c), holds(c - distance), distance, True))
+            pairs.append((holds(c), holds(c - distance), distance, True, False))
         else:
-            pairs.append((holds(c - distance), holds(c), -distance, False))
+            pairs.append((holds(c - distance), holds(c), -distance, False, whole))
         return len(pairs) - 1
 
     near = [pair(lambda who, d=d: (who >= 0) & (who + d < n_cp), d) for d in (1, 2)]
@@ -109,8 +104,9 @@
     for place, which, leg, rest in ASIDE:
         for goes, way in ((climbs, 1), (descends, -1)):
             go = functools.partial(goes, place=place)
-            outward[place, which, way] = pair(go, way * leg)
-            onward[place, which, way] = pair(lambda who, go=go, leg=way * leg: go(who - leg), way * rest)
+            outward[place, which, way] = pair(go, way * leg, True)
+            if rest:
+                onward[place, which, way] = pair(lambda who, go=go, leg=way * leg: go(who - leg), way * rest)
 
     barrier = pltpu.get_barrier_semaphore()
     for offset in range(1, n_tp):
@@ -118,14 +114,16 @@
             barrier, inc=1, device_id=(c, peer(offset, 1)), device_id_type=MESH
         )
     greeted = n_tp - 1
-    for is_lower, is_upper, distance, _ in pairs:
-        greeted = greeted + jnp.where(is_upper, 1, 0)
+
+    for is_lower, is_upper, distance, _, whole in pairs:
+        greeted = greeted + jnp.where(is_upper, n_tp if whole else 1, 0)
 
         @pl.when(is_lower)
         def _():
-            pl.semaphore_signal(
-                barrier, inc=1, device_id=(c + distance, t), device_id_type=MESH
-            )
+            for to in range(n_tp) if whole else (t,):
+                pl.semaphore_signal(
+                    barrier, inc=1, device_id=(c + distance, to), device_id_type=MESH
+                )
 
     def answered(number):
         @pl.when(pairs[number][0])
@@ -168,6 +166,13 @@
             dst[place] = in_place(place, lambda s: ref[s])
         own[which].start()
     pl.semaphore_wait(barrier, greeted)
+    for number, (_, is_upper, distance, sends, _) in enumerate(pairs):
+
+        @pl.when(is_upper & sends)
+        def _():
+            pl.semaphore_signal(
+                answer.at[number], inc=1, device_id=(c - distance, t), device_id_type=MESH
+            )
 
     kv_copies = ([], [])
     q_copies = {}
@@ -184,6 +189,49 @@
             )
             copy.start()
             kv_copies[which].append(copy)
+    def segment(place, below):
+        rows = pl.ds((LIST - below) * tokens, tokens)
+        return [k_all.at[place, rows], v_all.at[place, rows]]
+
+    low, high = segment(0, 0), segment(1, 0)
+    low_1, low_2, high_1, high_2 = segment(0, 1), segment(0, 2), segment(1, 1), segment(1, 2)
+    low_1_in, low_2_in, high_1_in, high_2_in = [
+        [far_recv.at[i, which] for which in range(2)] for i in range(4)
+    ]
+    aside, aside_in = [relay.at[0], relay.at[1]], [relay_recv.at[0], relay_recv.at[1]]
+
+    edge = GROUP - 1
+    crossing = {1: [], -1: []}
+    for number, (place, which, leg, rest) in enumerate(ASIDE):
+        for goes, way, side in ((climbs, 1, 0), (descends, -1, 1)):
+            dst, recv = aside[which], aside_in[which]
+            if not rest:
+                dst, recv = ((low_1, low_1_in), (high_1, high_1_in))[side]
+                dst, recv = dst[which], recv[which]
+            copies = [
+                pltpu.make_async_remote_copy(
+                    src_ref=(k_cut, v_cut)[which].at[side, :, pl.ds(to * kv_width, kv_width)],
+                    dst_ref=dst.at[own_rows],
+                    send_sem=cross_send.at[number, to],
+                    recv_sem=recv,
+                    device_id=(c + way * leg, to),
+                    device_id_type=MESH,
+                )
+                for to in range(n_tp)
+            ]
+            crossing[way].append((goes(c, place), (place, which, way), copies))
+
+    def cross(way):
+        for when, key, copies in crossing[way]:
+            if way > 0:
+                answered(outward[key])
+
+            @pl.when(when)
+            def _():
+                for copy in copies:
+                    copy.start()
+
+    cross(-1)
     for offset in ORDER:
         to = peer(offset, 1)
         q_copies[offset] = pltpu.make_async_remote_copy(
@@ -194,16 +242,22 @@
             device_id=(c, to),
             device_id_type=MESH,
         )
+
+    crosses_up = (c + GROUP < n_cp) & (c % GROUP >= edge - 1)
     for offset in ORDER[:AHEAD]:
         q_copies[offset].start()
 
-    for number, (is_lower, is_upper, distance, sends) in enumerate(pairs):
-
-        @pl.when(is_upper & sends)
-        def _():
-            pl.semaphore_signal(
-                answer.at[number], inc=1, device_id=(c - distance, t), device_id_type=MESH
-            )
+    @pl.when(~crosses_up)
+    def _():
+        for offset in ORDER[AHEAD:]:
+            q_copies[offset].start()
+
+    cross(1)
+
+    @pl.when(crosses_up)
+    def _():
+        for offset in ORDER[AHEAD:]:
+            q_copies[offset].start()
 
     for copy in small[1:]:
         copy.wait()
@@ -220,10 +274,6 @@
             low_bound[place, at : at + 128, :] = jnp.broadcast_to(
                 row[:, at : at + 128], (128, 128)
             ).T
-
-    def segment(place, below):
-        rows = pl.ds((LIST - below) * tokens, tokens)
-        return [k_all.at[place, rows], v_all.at[place, rows]]
 
     def far(which, src, dst, order, recv, distance):
         return pltpu.make_async_remote_copy(
@@ -235,53 +285,40 @@
             device_id_type=MESH,
         )
 
-    low, high = segment(0, 0), segment(1, 0)
-    low_1, low_2, high_1, high_2 = segment(0, 1), segment(0, 2), segment(1, 1), segment(1, 2)
-    low_1_in, low_2_in, high_1_in, high_2_in = [
-        [far_recv.at[i, which] for which in range(2)] for i in range(4)
-    ]
-    aside, aside_in = [relay.at[0], relay.at[1]], [relay_recv.at[0], relay_recv.at[1]]
     last = c == n_cp - 1
-    late = (c % GROUP == 0) | ((c % GROUP == GROUP - 1) & ~last)
     hand_low, hand_high = even & (c >= 2), odd
-    both, edge = (0, 1), GROUP - 1
+    both = (0, 1)
     first = [
-        ((0,), c + 1 < n_cp, low, low_1, low_1_in, 1),
-        ((1,), (c + 1 < n_cp) & ~climbs(c, edge), low, low_1, low_1_in, 1),
-        ((0,), c >= 1, high, high_1, high_1_in, -1),
-        ((1,), (c >= 1) & ~descends(c, edge), high, high_1, high_1_in, -1),
+        (both, (c + 1 < n_cp) & ~climbs(c, edge), low, low_1, low_1_in, 1),
+        (both, (c >= 1) & ~descends(c, edge), high, high_1, high_1_in, -1),
         (both, even & (c + 2 < n_cp) & ~climbs(c, edge - 1), low, low_2, low_2_in, 2),
         (both, odd & (c >= 2) & ~descends(c, edge - 1), high, high_2, high_2_in, -2),
     ]
     passed = []
     for place, which, leg, rest in ASIDE:
-        first += [
-            ((which,), climbs(c, place), low, aside, aside_in, leg),
-            ((which,), descends(c, place), high, aside, aside_in, -leg),
-        ]
-        to_low, to_high = (low_1, high_1) if place == edge else (low_2, high_2)
-        in_low, in_high = (low_1_in, high_1_in) if place == edge else (low_2_in, high_2_in)
-        passed += [
-            ((which,), climbs(c - leg, place), aside, to_low, in_low, rest),
-            ((which,), descends(c + leg, place), aside, to_high, in_high, -rest),
-        ]
+        if rest:
+            to_low, to_high = (low_1, high_1) if place == edge else (low_2, high_2)
+            in_low, in_high = (low_1_in, high_1_in) if place == edge else (low_2_in, high_2_in)
+            passed += [
+                ((which,), climbs(c - leg, place), aside, to_low, in_low, rest),
+                ((which,), descends(c + leg, place), aside, to_high, in_high, -rest),
+            ]
     handed = [
         (both, hand_low, low_1, low_2, low_2_in, 1),
         (both, hand_high, high_1, high_2, high_2_in, -1),
     ]
     moves = [(order,) + move for order, move in enumerate(first + passed + handed)]
-    ways = [key + (way,) for key in ((a[0], a[1]) for a in ASIDE) for way in (1, -1)]
-    waits = {len(first) - len(ways) + i: outward[key] for i, key in enumerate(ways)}
-    waits.update({len(first) + i: onward[key] for i, key in enumerate(ways)})
+    ways = [(place, which, way) for place, which, _, rest in ASIDE if rest for way in (1, -1)]
+    waits = {len(first) + i: onward[key] for i, key in enumerate(ways)}
     first, passed, handed = moves[: len(first)], moves[len(first) : -2], moves[-2:]
 
-    def send(move, which, also=True):
+    def send(move, which):
         order, whiches, when, src, dst, recv, distance = move
         if which in whiches:
             if order in waits and distance > 0:
                 answered(waits[order])
 
-            @pl.when(when & also)
+            @pl.when(when)
             def _():
                 far(which, src, dst, order, recv, distance).start()
 
@@ -290,11 +327,11 @@
         def _():
             far(which, dst, dst, 0, recv, 0).wait_recv()
 
-    def hand_on(which, also):
-        arrive(hand_low & also, which, low_1, low_1_in)
-        arrive(hand_high & ~last & also, which, high_1, high_1_in)
+    def hand_on(which):
+        arrive(hand_low, which, low_1, low_1_in)
+        arrive(hand_high & ~last, which, high_1, high_1_in)
         for move in handed:
-            send(move, which, also)
+            send(move, which)
 
     for which in range(2):
         own[which].wait()
@@ -309,9 +346,6 @@
         for move in first:
             if move[-1] > 0:
                 send(move, which)
-    for offset in ORDER[AHEAD:]:
-        q_copies[offset].start()
-
     for which in range(2):
 
         @pl.when(c < 1)
@@ -327,11 +361,12 @@
             high_1[which][...] = low[which][...]
 
     for which in range(2):
-        hand_on(which, ~late)
         for move in passed:
             if which in move[1]:
                 arrive(move[2], which, aside, aside_in)
             send(move, which)
+    for which in range(2):
+        hand_on(which)
 
     place_a = jnp.where(c % GROUP < 2, 1, 0)
     place_b = 1 - place_a
@@ -388,30 +423,39 @@
     own[2].wait()
     keys_in(place_a)
     arrived = {0}
-    for turn, offsets in SCHEDULE:
-        if turn == "hand":
-            for which in range(2):
-                hand_on(which, late)
-            continue
-        if turn == "keys":
+    for step in SCHEDULE:
+        if step == "keys":
             keys_in(place_b)
             continue
-        for offset in offsets:
-            if offset not in arrived:
-                arrived.add(offset)
-                q_copies[offset].wait_recv()
-        start, size, half = part_of(offsets)
-        rows = pl.ds(pl.multiple_of(start, size), size)
-        if turn == "a":
-            done[rows, :] = attend(place_a, start, size, half)
-        else:
-            result_a, result_b = done[rows, :], attend(place_b, start, size, half)
-            b_is_0 = swapped == (place_b == 1)
-            out_ref[0, rows, :] = jnp.where(b_is_0, result_b, result_a)
-            out_ref[1, rows, :] = jnp.where(b_is_0, result_a, result_b)
+        for _, offsets in step:
+            for offset in offsets:
+                if offset not in arrived:
+                    arrived.add(offset)
+                    q_copies[offset].wait_recv()
+        results = {}
+        for turn, offsets in step:
+            place = place_a if turn == "a" else place_b
+            start, size, half = part_of(offsets)
+            results[turn, offsets] = start, size, attend(place, start, size, half)
+        for (turn, offsets), (start, size, result) in results.items():
+            rows = pl.ds(pl.multiple_of(start, size), size)
+            if turn == "b":
+                result_a = results["a", offsets][2] if ("a", offsets) in results else done[rows, :]
+                b_is_0 = swapped == (place_b == 1)
+                out_ref[0, rows, :] = jnp.where(b_is_0, result, result_a)
+                out_ref[1, rows, :] = jnp.where(b_is_0, result_a, result)
+            elif ("b", offsets) not in results:
+                done[rows, :] = result
 
     for copy in kv_copies[0] + kv_copies[1] + list(q_copies.values()):
         copy.wait_send()
+    for when, _, copies in crossing[1] + crossing[-1]:
+
+        @pl.when(when)
+        def _():
+            for copy in copies:
+                copy.wait_send()
+
     for order, whiches, when, src, dst, recv, distance in moves:
 
         @pl.when(when)
@@ -458,6 +502,7 @@
             dma((8 + 4 * len(ASIDE), 2)),
             dma((4, 2)),
             dma((2,)),
+            dma((len(ASIDE), n_tp)),
             pltpu.SemaphoreType.REGULAR((2 + 4 * len(ASIDE),)),
         ],
         compiler_params=pltpu.CompilerParams(

time: 29.1 us -> 28.5 us (0.979)
  the two profiles are of different devices: /device:TPU:184 before, /device:TPU:326 now
where the time goes in v4:
time: 28.5 us; the launch traced here: 28.4 us
  Pallas kernels  27.4 us (96%)
  local copies, waits for them, and re-layouts  0.97 us (3%)
    pallas_call x1, Pallas kernels, on_device(): pl.pallas_call(functools.partial(kernel, n_cp, n_tp), out_shape=pltpu.VME...  27.4 us
    unnamed x1, local copies, waits for them, and re-layouts  0.97 us

profile of v4, /device:TPU:326, one launch (start us, length us, event | category | flops | bytes accessed | tf_op | source)
XLA Modules:
  0.0 28.4 jit_solution(18360874952624472269)
XLA Ops:
  0.0 27.4 %attention.1 = bf16[2,256,1024]{2,1,0:T(8,128)(2,1)S(1)} custom-call(bf16[2,32,8192]{2,1,0:T(8,128)(2,1)} %q_hbm.1, bf16[2,32,1024]{2,1,0:T(8,128)(2,1)} %k_hbm.1, bf16[2,32,1024]{2,1,0:T(8,128)(2,1)} %v_hbm.1, s32[2,256]{1,0:T(2,128)} %start_hbm.1, s32[2,2]{1,0:T(2,128)} %list_hbm.1, s32[128]{0:T(128)} %slot_hbm.1), custom_call_target="tpu_custom_call" | custom-call | tf_op jit(solution)/shard_map/attention/pallas_call | solution.py:476
  27.4 1.0 %copy.8 = bf16[2,256,1024]{2,1,0:T(8,128)(2,1)} copy(bf16[2,256,1024]{2,1,0:T(8,128)(2,1)S(1)} %attention.1) | data formatting | bytes 2097152

commit v5 on v4

--- a/solution.py
+++ b/solution.py
@@ -23,11 +23,10 @@
     "keys",
     (("b", (0, 1)), ("b", (2, 3))),
     (("a", (6, 7)), ("b", (6, 7))),
-    (("a", (4,)), ("b", (4,))),
-    (("a", (5,)), ("b", (5,))),
+    (("a", (4, 5)), ("b", (4, 5))),
 )
 GROUP = 16
-ASIDE = ((14, 0, 16, -14), (14, 1, 14, -12), (15, 0, 1, 0), (15, 1, 3, -2))
+ASIDE = ((15, 0, 1, 0), (15, 1, 1, 0), (14, 0, 16, -14), (14, 1, 14, -12))
 
 
 def kernel(
@@ -423,7 +422,26 @@
     own[2].wait()
     keys_in(place_a)
     arrived = {0}
+    def all_but_queries_sent():
+        for copy in kv_copies[0] + kv_copies[1]:
+            copy.wait_send()
+        for when, _, copies in crossing[1] + crossing[-1]:
+
+            @pl.when(when)
+            def _():
+                for copy in copies:
+                    copy.wait_send()
+
+        for order, whiches, when, src, dst, recv, distance in moves:
+
+            @pl.when(when)
+            def _():
+                for which in whiches:
+                    far(which, src, dst, order, recv, distance).wait_send()
+
     for step in SCHEDULE:
+        if step is SCHEDULE[-1]:
+            all_but_queries_sent()
         if step == "keys":
             keys_in(place_b)
             continue
@@ -447,21 +465,8 @@
             elif ("b", offsets) not in results:
                 done[rows, :] = result
 
-    for copy in kv_copies[0] + kv_copies[1] + list(q_copies.values()):
+    for copy in q_copies.values():
         copy.wait_send()
-    for when, _, copies in crossing[1] + crossing[-1]:
-
-        @pl.when(when)
-        def _():
-            for copy in copies:
-                copy.wait_send()
-
-    for order, whiches, when, src, dst, recv, distance in moves:
-
-        @pl.when(when)
-        def _():
-            for which in whiches:
-                far(which, src, dst, order, recv, distance).wait_send()
 
 
 def on_device(n_cp, n_tp, *operands):

time: 28.5 us -> 28.5 us (level)
  the two profiles are of different devices: /device:TPU:326 before, /device:TPU:184 now
where the time goes in v5:
time: 28.5 us; the launch traced here: 28.4 us
  Pallas kernels  27.4 us (96%)
  local copies, waits for them, and re-layouts  0.97 us (3%)
    pallas_call x1, Pallas kernels, on_device(): pl.pallas_call(functools.partial(kernel, n_cp, n_tp), out_shape=pltpu.VME...  27.4 us
    unnamed x1, local copies, waits for them, and re-layouts  0.97 us

profile of v5, /device:TPU:184, one launch (start us, length us, event | category | flops | bytes accessed | tf_op | source)
XLA Modules:
  0.0 28.4 jit_solution(8810443266874093886)
XLA Ops:
  0.0 27.4 %attention.1 = bf16[2,256,1024]{2,1,0:T(8,128)(2,1)S(1)} custom-call(bf16[2,32,8192]{2,1,0:T(8,128)(2,1)} %q_hbm.1, bf16[2,32,1024]{2,1,0:T(8,128)(2,1)} %k_hbm.1, bf16[2,32,1024]{2,1,0:T(8,128)(2,1)} %v_hbm.1, s32[2,256]{1,0:T(2,128)} %start_hbm.1, s32[2,2]{1,0:T(2,128)} %list_hbm.1, s32[128]{0:T(128)} %slot_hbm.1), custom_call_target="tpu_custom_call" | custom-call | tf_op jit(solution)/shard_map/attention/pallas_call | solution.py:481
  27.4 1.0 %copy.8 = bf16[2,256,1024]{2,1,0:T(8,128)(2,1)} copy(bf16[2,256,1024]{2,1,0:T(8,128)(2,1)S(1)} %attention.1) | data formatting | bytes 2097152

commit v6 on v5

--- a/solution.py
+++ b/solution.py
@@ -26,7 +26,7 @@
     (("a", (4, 5)), ("b", (4, 5))),
 )
 GROUP = 16
-ASIDE = ((15, 0, 1, 0), (15, 1, 1, 0), (14, 0, 16, -14), (14, 1, 14, -12))
+ASIDE = ((14, 0, 16, -14), (14, 1, 14, -12), (15, 0, 1, 0), (15, 1, 3, -2))
 
 
 def kernel(

time: 28.5 us -> 28 us (0.982)
  the two profiles are of different devices: /device:TPU:184 before, /device:TPU:326 now
where the time goes in v6:
time: 28 us; the launch traced here: 27.9 us
  Pallas kernels  26.9 us (96%)
  local copies, waits for them, and re-layouts  0.97 us (3%)
    pallas_call x1, Pallas kernels, on_device(): pl.pallas_call(functools.partial(kernel, n_cp, n_tp), out_shape=pltpu.VME...  26.9 us
    unnamed x1, local copies, waits for them, and re-layouts  0.97 us

profile of v6, /device:TPU:326, one launch (start us, length us, event | category | flops | bytes accessed | tf_op | source)
XLA Modules:
  0.0 27.9 jit_solution(1410490331592829376)
XLA Ops:
  0.0 26.9 %attention.1 = bf16[2,256,1024]{2,1,0:T(8,128)(2,1)S(1)} custom-call(bf16[2,32,8192]{2,1,0:T(8,128)(2,1)} %q_hbm.1, bf16[2,32,1024]{2,1,0:T(8,128)(2,1)} %k_hbm.1, bf16[2,32,1024]{2,1,0:T(8,128)(2,1)} %v_hbm.1, s32[2,256]{1,0:T(2,128)} %start_hbm.1, s32[2,2]{1,0:T(2,128)} %list_hbm.1, s32[128]{0:T(128)} %slot_hbm.1), custom_call_target="tpu_custom_call" | custom-call | tf_op jit(solution)/shard_map/attention/pallas_call | solution.py:481
  26.9 1.0 %copy.8 = bf16[2,256,1024]{2,1,0:T(8,128)(2,1)} copy(bf16[2,256,1024]{2,1,0:T(8,128)(2,1)S(1)} %attention.1) | data formatting | bytes 2097152
